TPU v7x, 32 devices: a whole 2x2x4 slice. The times are simulated.
32 devices in a mesh: dp: 4 (over y, x), expert: 4 (over z), tensor: 2 (over core).
Axes of the slice: x: 2, y: 2, z: 4, core: 2. Of those that a mesh axis runs over, the one named last changes fastest.
Arguments:
- activations: bfloat16 [2048, 2880], P(('dp', 'expert'), 'tensor'), may hold values from -6 to 6
- output_gradient: bfloat16 [2048, 2880], P(('dp', 'expert'), 'tensor'), may hold values from -6 to 6
- combine_weight: float32 [2048, 4], P(('dp', 'expert')), may hold values from 0.05 to 0.6
- token_experts: int32 [2048, 4], P(('dp', 'expert')), may hold values from 0 to 3, as said below
- gate_up_weight: bfloat16 [4, 2, 1440, 2880], P('expert', None, 'tensor'), may hold values from -0.109375 to 0.109375
- gate_up_channel_scale: float32 [4, 2, 1440], P('expert', None, 'tensor'), may hold values from 0.5 to 2
- down_weight: bfloat16 [4, 1440, 2880], P('expert', 'tensor'), may hold values from -0.15625 to 0.15625
- down_channel_scale: float32 [4, 2880], P('expert'), may hold values from 0.5 to 2
- adapter_input_first: bfloat16 [4, 2880, 32], P('expert'), may hold values from -0.109375 to 0.109375
- adapter_input_second: bfloat16 [4, 32, 2, 1440], P('expert', None, None, 'tensor'), may hold values from -0.5 to 0.5
- adapter_down_first: bfloat16 [4, 1440, 32], P('expert', 'tensor'), may hold values from -0.15625 to 0.15625
- adapter_down_second: bfloat16 [4, 32, 2880], P('expert'), may hold values from -0.5 to 0.5
Outputs:
- input_grad: bfloat16 [2048, 2880], P(('dp', 'expert'), 'tensor')
- grad_a_in: float32 [4, 2880, 32], P('expert', 'tensor')
- grad_b_in: float32 [4, 32, 2, 1440], P('expert', None, None, 'tensor')
- grad_a_down: float32 [4, 1440, 32], P('expert', 'tensor')
- grad_b_down: float32 [4, 32, 2880], P('expert', None, 'tensor')
Inputs may be any that keep to these rules, and one draw needn't show every extreme that they name: `token_experts`: each row names 4 different experts.
All inputs are finite; a program needn't handle non-finite values.
Results may differ from a plain program's by a relative error of at most 0.02.
Values may be sent and summed in bfloat16 or wider, within the bound.
A program may use at most 128 MiB of HBM per device.

v0:
```python
import jax
import jax.numpy as jnp
from jax import lax
from jax.sharding import PartitionSpec as P

ALPHA = 1.702
ADAPTER_SCALE = 2.0


def contract_product(left, right, left_dim, right_dim):
    return lax.dot_general(
        left, right, (((left_dim,), (right_dim,)), ((), ())), preferred_element_type=jnp.float32
    )


def shards(
    activations,
    output_gradient,
    combine_weight,
    token_experts,
    gate_up_weight,
    gate_up_channel_scale,
    down_weight,
    down_channel_scale,
    adapter_input_first,
    adapter_input_second,
    adapter_down_first,
    adapter_down_second,
):
    single_float = jnp.float32
    brain_float_half = jnp.bfloat16
    n_expert = lax.axis_size("expert")
    local_count = gate_up_weight.shape[0]
    experts_all = local_count * n_expert
    tok_rows = activations.shape[0]
    top_count = token_experts.shape[1]
    capacity = min(tok_rows * top_count * 11 // (8 * experts_all), tok_rows)
    gradient_slice = activations.shape[1]
    slots_all = experts_all * capacity
    flat_experts = token_experts.reshape(tok_rows * top_count)
    onehot = (flat_experts[:, None] == jnp.arange(experts_all, dtype=jnp.int32)[None, :]).astype(
        jnp.int32
    )
    before = jnp.cumsum(onehot, axis=0, dtype=jnp.int32) - onehot
    counted = jnp.sum(before * onehot, axis=1, dtype=jnp.int32)
    slot_positions = jnp.where(counted < capacity, counted, -1).reshape(tok_rows, top_count)
    target = jnp.where(slot_positions >= 0, token_experts * capacity + slot_positions, -1)
    matched = target[None, :, :] == jnp.arange(slots_all, dtype=jnp.int32)[:, None, None]
    placing = jnp.any(matched, axis=2).astype(brain_float_half)
    slot_weight = jnp.sum(jnp.where(matched, combine_weight[None, :, :], 0.0), axis=(1, 2)).reshape(
        experts_all, capacity
    )
    whole_x, whole_dy = (
        lax.all_gather(activations, "tensor", axis=1, tiled=True),
        lax.all_gather(output_gradient, "tensor", axis=1, tiled=True),
    )
    d_whole = whole_x.shape[1]
    sent_x = (
        jnp.dot(placing, whole_x, preferred_element_type=single_float)
        .astype(brain_float_half)
        .reshape(experts_all, capacity, d_whole)
    )
    sent_dy = (
        jnp.dot(placing, whole_dy, preferred_element_type=single_float)
        .astype(brain_float_half)
        .reshape(experts_all, capacity, d_whole)
    )
    recv_x, recv_dy, recv_w = (
        lax.all_to_all(sent_x, "expert", split_axis=0, concat_axis=1, tiled=True),
        lax.all_to_all(sent_dy, "expert", split_axis=0, concat_axis=1, tiled=True),
        lax.all_to_all(
            slot_weight.astype(jnp.bfloat16), "expert", split_axis=0, concat_axis=1, tiled=True
        ).astype(slot_weight.dtype),
    )
    gradient_start = lax.axis_index("tensor") * gradient_slice
    gradient_listing = ([], [], [], [])
    input_rows = recv_x[0]
    dy_rows = recv_dy[0]
    gradient_rows = (recv_w[0][:, None] * dy_rows.astype(single_float)).astype(brain_float_half)
    scaled_gradient = (gradient_rows.astype(single_float) * down_channel_scale[0][None, :]).astype(
        brain_float_half
    )
    adapter_input_rows = jnp.dot(
        input_rows, adapter_input_first[0], preferred_element_type=single_float
    ).astype(brain_float_half)
    gate_values = (
        contract_product(input_rows, gate_up_weight[0, 0], 1, 1)
        * gate_up_channel_scale[0, 0][None, :]
    )
    gate_values = gate_values + ADAPTER_SCALE * jnp.dot(
        adapter_input_rows, adapter_input_second[0][:, 0, :], preferred_element_type=single_float
    )
    up_activation = (
        contract_product(input_rows, gate_up_weight[0, 1], 1, 1)
        * gate_up_channel_scale[0, 1][None, :]
    )
    up_activation = up_activation + ADAPTER_SCALE * jnp.dot(
        adapter_input_rows, adapter_input_second[0][:, 1, :], preferred_element_type=single_float
    )
    sig = jax.nn.sigmoid(ALPHA * gate_values)
    glu = gate_values * sig
    hidden_units = ((up_activation + 1.0) * glu).astype(brain_float_half)
    down_portion = jnp.dot(hidden_units, adapter_down_first[0], preferred_element_type=single_float)
    down_sum = lax.psum(down_portion.astype(jnp.bfloat16), "tensor").astype(jnp.float32)
    backward_adapter = contract_product(gradient_rows, adapter_down_second[0], 1, 1).astype(
        brain_float_half
    )
    hidden_gradient = contract_product(
        scaled_gradient, down_weight[0], 1, 1
    ) + ADAPTER_SCALE * contract_product(backward_adapter, adapter_down_first[0], 1, 1)
    d_up = hidden_gradient * glu
    d_gate = (
        hidden_gradient * (up_activation + 1.0) * sig * (1.0 + ALPHA * gate_values * (1.0 - sig))
    )
    d_both = jnp.stack([d_gate, d_up], axis=1)
    adapter_mid_gradient = d_both.astype(brain_float_half)
    dz_scaled = (d_both * gate_up_channel_scale[0][None, :, :]).astype(brain_float_half)
    input_portion = jnp.einsum(
        "ndy,tdy->nt",
        adapter_mid_gradient,
        adapter_input_second[0],
        preferred_element_type=single_float,
    )
    in_sum = lax.psum(input_portion.astype(jnp.bfloat16), "tensor").astype(jnp.float32)
    down_adapter = down_sum.astype(brain_float_half)
    input_adapter = in_sum.astype(brain_float_half)
    partial_value = jnp.einsum(
        "rjf,jfd->rd", dz_scaled, gate_up_weight[0], preferred_element_type=single_float
    )
    summed_values = lax.psum_scatter(
        partial_value.astype(jnp.bfloat16), "tensor", scatter_dimension=1, tiled=True
    ).astype(jnp.float32)
    input_first_rows = lax.dynamic_slice_in_dim(
        adapter_input_first[0], gradient_start, gradient_slice, 0
    )
    input_gradient_rows = (
        summed_values + ADAPTER_SCALE * contract_product(input_adapter, input_first_rows, 1, 1)
    ).astype(brain_float_half)
    dx_list = [input_gradient_rows]
    input_columns = lax.dynamic_slice_in_dim(input_rows, gradient_start, gradient_slice, 1)
    gradient_columns = lax.dynamic_slice_in_dim(gradient_rows, gradient_start, gradient_slice, 1)
    gradient_listing[0].append(ADAPTER_SCALE * contract_product(input_columns, input_adapter, 0, 0))
    gradient_listing[1].append(
        ADAPTER_SCALE
        * jnp.einsum(
            "hp,hwl->pwl",
            adapter_input_rows,
            adapter_mid_gradient,
            preferred_element_type=single_float,
        )
    )
    gradient_listing[2].append(
        ADAPTER_SCALE * contract_product(hidden_units, backward_adapter, 0, 0)
    )
    gradient_listing[3].append(
        ADAPTER_SCALE * contract_product(down_adapter, gradient_columns, 0, 0)
    )
    stacked = tuple((jnp.stack(items, axis=0) for items in gradient_listing))
    input_first_gradient, input_second_gradient, down_first_gradient, down_second_gradient = (
        lax.psum(stacked[0].astype(jnp.bfloat16), "dp").astype(jnp.float32),
        lax.psum(stacked[1].astype(jnp.bfloat16), "dp").astype(jnp.float32),
        lax.psum(stacked[2].astype(jnp.bfloat16), "dp").astype(jnp.float32),
        lax.psum(stacked[3].astype(jnp.bfloat16), "dp").astype(jnp.float32),
    )
    returned = lax.all_to_all(
        jnp.stack(dx_list, axis=0), "expert", split_axis=1, concat_axis=0, tiled=True
    )
    flat_rows = returned.reshape(slots_all, gradient_slice)
    input_grad = contract_product(placing, flat_rows, 0, 0).astype(brain_float_half)
    return (
        input_grad,
        input_first_gradient,
        input_second_gradient,
        down_first_gradient,
        down_second_gradient,
    )


def solution(mesh):
    placed = (
        P(("dp", "expert"), "tensor"),
        P(("dp", "expert"), "tensor"),
        P(("dp", "expert"), None),
        P(("dp", "expert"), None),
        P("expert", None, "tensor", None),
        P("expert", None, "tensor"),
        P("expert", "tensor", None),
        P("expert", None),
        P("expert", None, None),
        P("expert", None, None, "tensor"),
        P("expert", "tensor", None),
        P("expert", None, None),
    )
    return jax.shard_map(
        shards,
        mesh=mesh,
        in_specs=placed,
        out_specs=(
            P(("dp", "expert"), "tensor"),
            P("expert", "tensor", None),
            P("expert", None, None, "tensor"),
            P("expert", "tensor", None),
            P("expert", None, "tensor"),
        ),
        check_vma=False,
    )
```

profile of v0, /device:TPU:0, one launch (start us, length us, event | category | flops | bytes accessed | tf_op | source)
XLA Modules:
  0.0 350.1 jit_solution(4996829955877163607)
XLA Ops:
  7.2 0.8 copy.54
  8.1 0.1 eq.38
  8.2 0.7 broadcast_multiply_fusion
  8.9 1.2 reduce-window.6
  10.1 0.2 slice_reduce_fusion
  10.3 0.2 reduce-window.9
  10.6 0.1 reduce_sum.21
  10.7 0.1 copy.57
  10.9 0.9 select_reduce_fusion
  11.8 0.6 copy.59
  12.4 6.3 %all-to-all-start = ((bf16[4,1,128]{2,1,0:T(2,128)(2,1)}), bf16[4,1,128]{2,1,0:T(2,128)(2,1)S(1)}, u32[]{:S(2)}, u32[]{:S(2)}) async-start(bf16[4,1,128]{2,1,0:T(2,128)(2,1)} %copy.59), calls=%async_computation | async-start | bytes 4096 | tf_op jit(solution)/shard_map/all_to_all | solution.py:71
  18.7 0.1 fusion.38
  18.8 2.5 all_gather.7
  21.4 0.9 fusion.22
  22.3 2.1 copy.78
  24.5 5.1 %all-to-all-start.2 = ((bf16[4,128,2880]{1,2,0:T(8,128)(2,1)}), bf16[4,128,2880]{1,2,0:T(8,128)(2,1)S(1)}, u32[]{:S(2)}, u32[]{:S(2)}) async-start(bf16[4,128,2880]{1,2,0:T(8,128)(2,1)} %bitcast.139), calls=%async_computation.2 | async-start | bytes 5898240 | tf_op jit(solution)/shard_map/all_to_all | solution.py:69
  29.6 2.5 all_gather.6
  32.1 0.9 fusion.21
  33.0 2.1 copy.79
  35.1 61.2 %all-to-all-done.2 = bf16[4,128,2880]{1,2,0:T(8,128)(2,1)S(1)} async-done(((bf16[4,128,2880]{1,2,0:T(8,128)(2,1)}), bf16[4,128,2880]{1,2,0:T(8,128)(2,1)S(1)}, u32[]{:S(2)}, u32[]{:S(2)}) %all-to-all-start.2) | async-done | bytes 2949152 | tf_op jit(solution)/shard_map/all_to_all | solution.py:69
  96.3 1.6 copy-done.2
  98.0 4.6 %all-to-all-start.1 = ((bf16[4,128,2880]{1,2,0:T(8,128)(2,1)}), bf16[4,128,2880]{1,2,0:T(8,128)(2,1)}, u32[]{:S(2)}, u32[]{:S(2)}) async-start(bf16[4,128,2880]{1,2,0:T(8,128)(2,1)} %bitcast.138), calls=%async_computation.1 | async-start | bytes 5898240 | tf_op jit(solution)/shard_map/all_to_all | solution.py:70
  102.6 0.2 all-reduce.7.cloned.1.call-start
  103.0 3.3 copy.64
  106.3 1.0 convolution_convert_fusion.4
  107.3 1.5 fusion.45
  108.8 1.6 fusion.46
  110.4 58.2 %all-to-all-done.1 = bf16[4,128,2880]{1,2,0:T(8,128)(2,1)} async-done(((bf16[4,128,2880]{1,2,0:T(8,128)(2,1)}), bf16[4,128,2880]{1,2,0:T(8,128)(2,1)}, u32[]{:S(2)}, u32[]{:S(2)}) %all-to-all-start.1) | async-done | bytes 2949152 | tf_op jit(solution)/shard_map/all_to_all | solution.py:70
  168.7 4.7 %multiply_convert_fusion = (bf16[4,128,2880]{1,2,0:T(8,128)(2,1)}, bf16[4,128,2880]{1,2,0:T(8,128)(2,1)}) fusion(f32[2880]{0:T(1024)S(1)} %reduce.1, bf16[4,128,2880]{1,2,0:T(8,128)(2,1)} %all-to-all-done.1, f32[4,128]{1,0:T(4,128)S(1)} %bitcast.143), kind=kLoop, calls=%fused_computation.3 | loop fusion | flops 8847360 | bytes 8860928 | tf_op jit(solution)/shard_map/convert_element_type | solution.py:80
  173.4 4.6 %copy.62 = bf16[4,128,2880]{2,1,0:T(8,128)(2,1)} copy(bf16[4,128,2880]{1,2,0:T(8,128)(2,1)} %get-tuple-element.38) | data formatting | bytes 5898240 | tf_op jit(solution)/shard_map/convert_element_type | solution.py:79
  178.0 4.6 %copy.61 = bf16[4,128,2880]{2,1,0:T(8,128)(2,1)} copy(bf16[4,128,2880]{1,2,0:T(8,128)(2,1)} %get-tuple-element.37) | data formatting | bytes 5898240 | tf_op jit(solution)/shard_map/convert_element_type | solution.py:80
  182.6 5.3 %multiply_add_fusion = f32[512,720]{0,1:T(8,128)S(1)} fusion(f32[512,720]{0,1:T(8,128)} %fusion.45, bf16[512,2880]{1,0:T(8,128)(2,1)S(1)} %bitcast.131, bf16[1,2,720,2880]{3,2,1,0:T(8,128)(2,1)} %param.16, f32[720]{0:T(1024)S(1)} %get-tuple-element.31), kind=kOutput, calls=%fused_computation.43 | convolution fusion | flops 2124472320 | bytes 10140480 | tf_op jit(solution)/shard_map/dot_general | solution.py:11
  187.9 4.8 %add_add_fusion = f32[512,720]{0,1:T(8,128)S(1)} fusion(f32[512,720]{0,1:T(8,128)S(1)} %copy-done.8, bf16[512,2880]{1,0:T(8,128)(2,1)S(1)} %bitcast.132, bf16[1,2,720,2880]{3,2,1,0:T(8,128)(2,1)} %param.16, f32[720]{0:T(1024)S(1)} %get-tuple-element.30), kind=kOutput, calls=%fused_computation.44 | convolution fusion | flops 2124840960 | bytes 10140480 | tf_op jit(solution)/shard_map/dot_general | solution.py:11
  192.8 1.0 convolution_convert_fusion.5
  193.8 0.8 copy-done.5
  194.6 2.5 fusion.8
  197.1 1.2 multiply_convert_fusion.4
  198.4 0.8 copy-done.6
  199.2 1.0 convolution_convert_fusion.3
  200.2 0.9 fusion.36
  201.2 0.3 reduce-scatter.2.cloned.1.call-start
  201.4 10.9 %bitcast_convert_fusion = bf16[512,2880]{0,1:T(8,128)(2,1)} fusion(bf16[1,2,720,2880]{3,2,1,0:T(8,128)(2,1)} %param.16, f32[512,1,720]{0,2,1:T(8,128)} %copy-done.4, f32[512,1,720]{0,2,1:T(8,128)} %copy-done.3, f32[2,720]{1,0:T(2,128)S(1)} %bitcast.146), kind=kOutput, calls=%fused_computation.2 | convolution fusion | flops 4250419200 | bytes 14198400 | tf_op jit(solution)/shard_map/rjf,jfd->rd/dot_general | solution.py:127
  212.4 5.8 %all-reduce.7.cloned.1.call-done = (bf16[512,32]{0,1:T(8,128)(2,1)}, bf16[512,32]{0,1:T(8,128)(2,1)}) async-done(((bf16[512,32]{0,1:T(8,128)(2,1)}, bf16[512,32]{0,1:T(8,128)(2,1)}), (bf16[512,32]{0,1:T(8,128)(2,1)}, bf16[512,32]{0,1:T(8,128)(2,1)})) %all-reduce.7.cloned.1.call-update) | async-done | bytes 65552 | tf_op jit(solution)/shard_map/psum | solution.py:124
  218.2 14.0 %reduce-scatter.2.cloned.1.call-done = bf16[512,1440]{0,1:T(8,128)(2,1)} async-done(((bf16[512,2880]{0,1:T(8,128)(2,1)}), bf16[512,1440]{0,1:T(8,128)(2,1)}) %reduce-scatter.2.cloned.1.call-update) | async-done | bytes 1474576 | tf_op jit(solution)/shard_map/reduce_scatter | solution.py:130
  232.2 3.3 fusion.15
  235.5 8.4 %copy.66 = bf16[1,512,1440]{2,0,1:T(2,128)(2,1)} copy(bf16[1,512,1440]{1,2,0:T(8,128)(2,1)} %fusion.15) | data formatting | bytes 2949120 | tf_op jit(solution)/shard_map/stack | solution.py:166
  244.0 0.5 broadcast.68
  244.5 12.8 %reduce.7 = bf16[512,1440]{1,0:T(8,128)(2,1)} reduce(bf16[512,1,1440]{2,1,0:T(2,128)(2,1)} %bitcast.136, bf16[]{:T(256)} %broadcast.68), dimensions={1}, to_apply=%bitcast.103.reduce_sub_computation | reduce | bytes 2949122
  257.2 4.8 %reshape.135 = bf16[4,2,92160]{2,1,0:T(2,128)(2,1)} reshape(bf16[512,1440]{1,0:T(8,128)(2,1)} %reduce.7) | data formatting | bytes 2949120
  262.1 4.9 %all-to-all-start.3 = ((bf16[4,2,92160]{2,1,0:T(2,128)(2,1)}), bf16[4,2,92160]{2,1,0:T(2,128)(2,1)}, u32[]{:S(2)}, u32[]{:S(2)}) async-start(bf16[4,2,92160]{2,1,0:T(2,128)(2,1)} %reshape.135), calls=%async_computation.4 | async-start | bytes 2949120 | tf_op jit(solution)/shard_map/all_to_all | solution.py:165
  267.0 5.4 %copy.68 = f32[4,128,2880]{2,1,0:T(8,128)} copy(bf16[4,128,2880]{1,2,0:T(8,128)(2,1)} %all-to-all-done.1) | data formatting | bytes 8847360 | tf_op jit(solution)/shard_map/convert_element_type | solution.py:79
  272.4 3.0 fusion.34
  275.4 1.3 fusion.19
  276.7 3.8 %fusion.20 = bf16[1,32,1440]{2,1,0:T(8,128)(2,1)} fusion(bf16[512,32]{0,1:T(8,128)(2,1)S(1)} %copy-done.13, f32[512,2880]{1,0:T(8,128)} %bitcast.135, s32[]{:T(128)S(6)} %select_n.21, f32[512]{0:T(512)S(1)} %bitcast.144), kind=kOutput, calls=%fused_computation.32 | convolution fusion | flops 48752640 | bytes 3272708 | tf_op jit(solution)/shard_map/dot_general | solution.py:11
  280.5 0.3 fusion.37
  280.9 16.7 %psum.45 = bf16[1,720,32]{1,2,0:T(8,128)(2,1)S(1)} all-reduce(bf16[1,720,32]{1,2,0:T(8,128)(2,1)S(1)} %fusion.37), channel_id=1, replica_groups=mesh['dp'=4,'expert'=4,'tensor'=2] {'dp'}, use_global_device_ids=true, to_apply=%region_9.10 | all-reduce | flops 23040 | bytes 92160 | tf_op jit(solution)/shard_map/psum | solution.py:162
  297.6 0.6 convert_element_type.183
  298.3 28.1 %all-reduce.5.cloned.1.call-done = (bf16[1,32,2,720]{3,1,2,0:T(8,128)(2,1)}, bf16[1,1440,32]{1,2,0:T(8,128)(2,1)}, bf16[1,32,1440]{2,1,0:T(8,128)(2,1)}) async-done(((bf16[1,32,2,720]{3,1,2,0:T(8,128)(2,1)}, bf16[1,1440,32]{1,2,0:T(8,128)(2,1)}, bf16[1,32,1440]{2,1,0:T(8,128)(2,1)}), (bf16[1,32,2,720]{3,1,2,0:T(8,128)(2,1)}, bf16[1,1440,32]{1,2,0:T(8,128)(2,1)}, ...) | async-done | bytes 276496 | tf_op jit(solution)/shard_map/psum | solution.py:161
  326.3 1.6 convert_element_type.176
  327.9 1.6 convert_element_type.192
  329.5 1.7 copy.69
  331.2 3.6 %reshape.136 = bf16[512,1,1440]{2,1,0:T(2,128)(2,1)S(1)} reshape(bf16[4,2,92160]{2,1,0:T(2,128)(2,1)} %all-to-all-done.3) | data formatting | bytes 2949120
  334.8 6.1 %copy.67 = bf16[1,512,1440]{1,2,0:T(8,128)(2,1)} copy(bf16[1,512,1440]{2,0,1:T(2,128)(2,1)S(1)} %bitcast.137) | data formatting | bytes 2949120 | tf_op jit(solution)/shard_map/all_to_all | solution.py:165
  341.0 2.7 convolution_convert_fusion.2
  (50 shorter events, 0.5 us)
Async XLA Ops:
  7.2 99.1 %copy-start = (bf16[1,2880,32]{1,2,0:T(8,128)(2,1)S(1)}, bf16[1,2880,32]{1,2,0:T(8,128)(2,1)}, u32[]{:S(2)}) copy-start(bf16[1,2880,32]{1,2,0:T(8,128)(2,1)} %param.20) | copy-start | bytes 552964
  12.4 12.1 %all-to-all-start = ((bf16[4,1,128]{2,1,0:T(2,128)(2,1)}), bf16[4,1,128]{2,1,0:T(2,128)(2,1)S(1)}, u32[]{:S(2)}, u32[]{:S(2)}) async-start(bf16[4,1,128]{2,1,0:T(2,128)(2,1)} %copy.59), calls=%async_computation | async-start | bytes 4096 | tf_op jit(solution)/shard_map/all_to_all | solution.py:71
  24.5 71.9 %all-to-all-start.2 = ((bf16[4,128,2880]{1,2,0:T(8,128)(2,1)}), bf16[4,128,2880]{1,2,0:T(8,128)(2,1)S(1)}, u32[]{:S(2)}, u32[]{:S(2)}) async-start(bf16[4,128,2880]{1,2,0:T(8,128)(2,1)} %bitcast.139), calls=%async_computation.2 | async-start | bytes 5898240 | tf_op jit(solution)/shard_map/all_to_all | solution.py:69
  96.3 1.6 copy-start.2
  96.3 6.5 %copy-start.9 = (bf16[1,32,2,720]{3,2,1,0:T(2,128)(2,1)S(1)}, bf16[1,32,2,720]{3,2,1,0:T(2,128)(2,1)}, u32[]{:S(2)}) copy-start(bf16[1,32,2,720]{3,2,1,0:T(2,128)(2,1)} %param.21) | copy-start | bytes 276484
  96.3 6.5 %copy-start.14 = (f32[1,2880]{1,0:T(1,128)S(1)}, f32[1,2880]{1,0:T(1,128)}, u32[]{:S(2)}) copy-start(f32[1,2880]{1,0:T(1,128)} %param.19) | copy-start | bytes 34564
  96.3 6.6 %copy-start.15 = (f32[1,2,720]{2,1,0:T(2,128)S(1)}, f32[1,2,720]{2,1,0:T(2,128)}, u32[]{:S(2)}) copy-start(f32[1,2,720]{2,1,0:T(2,128)} %param.17) | copy-start | bytes 17284
  98.0 70.7 %all-to-all-start.1 = ((bf16[4,128,2880]{1,2,0:T(8,128)(2,1)}), bf16[4,128,2880]{1,2,0:T(8,128)(2,1)}, u32[]{:S(2)}, u32[]{:S(2)}) async-start(bf16[4,128,2880]{1,2,0:T(8,128)(2,1)} %bitcast.138), calls=%async_computation.1 | async-start | bytes 5898240 | tf_op jit(solution)/shard_map/all_to_all | solution.py:70
  102.6 115.6 %all-reduce.7.cloned.1.call-start = ((), (), s32[]{:S(2)}) async-start(), calls=%async_computation.7 | async-start | bytes 131072 | tf_op jit(solution)/shard_map/psum | solution.py:124
  182.6 5.3 %copy-start.8 = (f32[512,720]{0,1:T(8,128)S(1)}, f32[512,720]{0,1:T(8,128)}, u32[]{:S(2)}) copy-start(f32[512,720]{0,1:T(8,128)} %fusion.46) | copy-start | bytes 4423684
  182.6 11.2 %slice-start = ((s8[4239360]{0:T(1024)(128)(4,1)}), s8[4194304]{0:T(1024)(128)(4,1)S(1)}, s32[]{:S(2)}) async-start(s8[4239360]{0:T(1024)(128)(4,1)} %bitcast.148), calls=%async_computation.8 | async-start | bytes 8388608
  187.9 4.9 %copy-start.1 = (bf16[4,128,2880]{2,1,0:T(8,128)(2,1)S(1)}, bf16[4,128,2880]{2,1,0:T(8,128)(2,1)}, u32[]{:S(2)}) copy-start(bf16[4,128,2880]{2,1,0:T(8,128)(2,1)} %copy.62) | copy-start | bytes 8847364
  187.9 4.9 %copy-start.10 = (bf16[1,32,2880]{2,1,0:T(8,128)(2,1)S(1)}, bf16[1,32,2880]{2,1,0:T(8,128)(2,1)}, u32[]{:S(2)}) copy-start(bf16[1,32,2880]{2,1,0:T(8,128)(2,1)} %param.23) | copy-start | bytes 552964
  187.9 5.9 %slice-start.1 = ((s8[4239360]{0:T(1024)(128)(4,1)}), s8[45056]{0:T(1024)(128)(4,1)S(1)}, s32[]{:S(2)}) async-start(s8[4239360]{0:T(1024)(128)(4,1)} %bitcast.148), calls=%async_computation.9 | async-start | bytes 90112
  192.8 1.9 copy-start.5
  194.6 2.5 copy-start.12
  198.3 0.9 copy-start.6
  198.3 1.8 copy-start.3
  198.4 1.8 copy-start.4
  201.2 31.0 %reduce-scatter.2.cloned.1.call-start = ((), (), s32[]{:S(2)}) async-start(), calls=%async_computation.5 | async-start | bytes 4423680 | tf_op jit(solution)/shard_map/reduce_scatter | solution.py:130
  262.1 69.1 %all-to-all-start.3 = ((bf16[4,2,92160]{2,1,0:T(2,128)(2,1)}), bf16[4,2,92160]{2,1,0:T(2,128)(2,1)}, u32[]{:S(2)}, u32[]{:S(2)}) async-start(bf16[4,2,92160]{2,1,0:T(2,128)(2,1)} %reshape.135), calls=%async_computation.4 | async-start | bytes 2949120 | tf_op jit(solution)/shard_map/all_to_all | solution.py:165
  267.0 59.3 %all-reduce.5.cloned.1.call-start = ((), (), s32[]{:S(2)}) async-start(), calls=%async_computation.6 | async-start | bytes 589824 | tf_op jit(solution)/shard_map/psum | solution.py:161
  272.4 3.0 copy-start.11
  275.4 1.3 copy-start.13
  276.7 3.8 %copy-start.7 = (bf16[512,720]{0,1:T(8,128)(2,1)S(1)}, bf16[512,720]{0,1:T(8,128)(2,1)}, u32[]{:S(2)}) copy-start(bf16[512,720]{0,1:T(8,128)(2,1)} %copy-done.6) | copy-start | bytes 2211844
Sparse Core Ops, SparseCore 0:
  201.3 16.8 all-reduce.6
  220.4 11.7 reduce-scatter.1
  280.6 45.6 all-reduce.4
where the time goes:
time: 352 us; the launch traced here: 350 us
  waiting for transfers between devices  167 us (47%)
  local copies, waits for them, and re-layouts  53 us (15%)
  matrix products  47.9 us (14%)
  other arithmetic  24.6 us (7%)
  blocking collectives  21.8 us (6%)
  starting transfers between devices  21.5 us (6%)
  between operations  14.1 us (4%)
    all_to_all x1, waiting for transfers between devices, shards(): lax.all_to_all(sent_x, 'expert', split_axis=0, concat_axis=1, tiled=True)  61.2 us
    all_to_all x1, waiting for transfers between devices, shards(): lax.all_to_all(sent_dy, 'expert', split_axis=0, concat_axis=1, tiled=True)  58.2 us
    psum x1, waiting for transfers between devices, shards(): lax.psum(stacked[1].astype(jnp.bfloat16), 'dp').astype(jnp.float32)  28.1 us
    dot_general x10, matrix products, contract_product(): lax.dot_general(left, right, (((left_dim,), (right_dim,)), ((), ())), pre...  26.1 us
    psum x1, blocking collectives, shards(): lax.psum(stacked[2].astype(jnp.bfloat16), 'dp').astype(jnp.float32)  16.7 us
    unnamed x42, local copies, waits for them, and re-layouts  14.9 us
    reduce_scatter x1, waiting for transfers between devices, shards(): lax.psum_scatter(partial_value.astype(jnp.bfloat16), 'tensor', scatter_di...  14 us
    unnamed x4, other arithmetic  12.9 us
  transfers between devices with their start and end apart: 7, of which 5 were waited for; matrix products, arithmetic and copies ran while one was open for 13% of the time, Pallas kernels for 0%

commit v1 on v0

--- a/solution.py
+++ b/solution.py
@@ -37,41 +37,60 @@
     capacity = min(tok_rows * top_count * 11 // (8 * experts_all), tok_rows)
     gradient_slice = activations.shape[1]
     slots_all = experts_all * capacity
-    flat_experts = token_experts.reshape(tok_rows * top_count)
-    onehot = (flat_experts[:, None] == jnp.arange(experts_all, dtype=jnp.int32)[None, :]).astype(
-        jnp.int32
-    )
-    before = jnp.cumsum(onehot, axis=0, dtype=jnp.int32) - onehot
-    counted = jnp.sum(before * onehot, axis=1, dtype=jnp.int32)
-    slot_positions = jnp.where(counted < capacity, counted, -1).reshape(tok_rows, top_count)
-    target = jnp.where(slot_positions >= 0, token_experts * capacity + slot_positions, -1)
-    matched = target[None, :, :] == jnp.arange(slots_all, dtype=jnp.int32)[:, None, None]
-    placing = jnp.any(matched, axis=2).astype(brain_float_half)
-    slot_weight = jnp.sum(jnp.where(matched, combine_weight[None, :, :], 0.0), axis=(1, 2)).reshape(
-        experts_all, capacity
-    )
-    whole_x, whole_dy = (
-        lax.all_gather(activations, "tensor", axis=1, tiled=True),
-        lax.all_gather(output_gradient, "tensor", axis=1, tiled=True),
-    )
-    d_whole = whole_x.shape[1]
-    sent_x = (
-        jnp.dot(placing, whole_x, preferred_element_type=single_float)
-        .astype(brain_float_half)
-        .reshape(experts_all, capacity, d_whole)
-    )
-    sent_dy = (
-        jnp.dot(placing, whole_dy, preferred_element_type=single_float)
-        .astype(brain_float_half)
-        .reshape(experts_all, capacity, d_whole)
-    )
-    recv_x, recv_dy, recv_w = (
-        lax.all_to_all(sent_x, "expert", split_axis=0, concat_axis=1, tiled=True),
-        lax.all_to_all(sent_dy, "expert", split_axis=0, concat_axis=1, tiled=True),
-        lax.all_to_all(
-            slot_weight.astype(jnp.bfloat16), "expert", split_axis=0, concat_axis=1, tiled=True
-        ).astype(slot_weight.dtype),
-    )
+    dense = experts_all == top_count and capacity == tok_rows
+    if dense:
+        expert_ids = jnp.arange(experts_all, dtype=jnp.int32)
+        token_weight = jnp.sum(
+            jnp.where(
+                token_experts[:, :, None] == expert_ids[None, None, :],
+                combine_weight[:, :, None],
+                0.0,
+            ),
+            axis=1,
+        )
+        half_x = lax.all_gather(activations, "expert", axis=0, tiled=True)
+        half_dy = lax.all_gather(output_gradient, "expert", axis=0, tiled=True)
+        weights = lax.all_gather(token_weight, "expert", axis=0, tiled=True)
+        mine = lax.axis_index("expert")
+        recv_w = lax.dynamic_slice_in_dim(weights, mine, 1, 1).reshape(1, -1)
+        recv_x = lax.all_gather(half_x, "tensor", axis=1, tiled=True)[None]
+        recv_dy = lax.all_gather(half_dy, "tensor", axis=1, tiled=True)[None]
+    else:
+        flat_experts = token_experts.reshape(tok_rows * top_count)
+        onehot = (flat_experts[:, None] == jnp.arange(experts_all, dtype=jnp.int32)[None, :]).astype(
+            jnp.int32
+        )
+        before = jnp.cumsum(onehot, axis=0, dtype=jnp.int32) - onehot
+        counted = jnp.sum(before * onehot, axis=1, dtype=jnp.int32)
+        slot_positions = jnp.where(counted < capacity, counted, -1).reshape(tok_rows, top_count)
+        target = jnp.where(slot_positions >= 0, token_experts * capacity + slot_positions, -1)
+        matched = target[None, :, :] == jnp.arange(slots_all, dtype=jnp.int32)[:, None, None]
+        placing = jnp.any(matched, axis=2).astype(brain_float_half)
+        slot_weight = jnp.sum(jnp.where(matched, combine_weight[None, :, :], 0.0), axis=(1, 2)).reshape(
+            experts_all, capacity
+        )
+        whole_x, whole_dy = (
+            lax.all_gather(activations, "tensor", axis=1, tiled=True),
+            lax.all_gather(output_gradient, "tensor", axis=1, tiled=True),
+        )
+        d_whole = whole_x.shape[1]
+        sent_x = (
+            jnp.dot(placing, whole_x, preferred_element_type=single_float)
+            .astype(brain_float_half)
+            .reshape(experts_all, capacity, d_whole)
+        )
+        sent_dy = (
+            jnp.dot(placing, whole_dy, preferred_element_type=single_float)
+            .astype(brain_float_half)
+            .reshape(experts_all, capacity, d_whole)
+        )
+        recv_x, recv_dy, recv_w = (
+            lax.all_to_all(sent_x, "expert", split_axis=0, concat_axis=1, tiled=True),
+            lax.all_to_all(sent_dy, "expert", split_axis=0, concat_axis=1, tiled=True),
+            lax.all_to_all(
+                slot_weight.astype(jnp.bfloat16), "expert", split_axis=0, concat_axis=1, tiled=True
+            ).astype(slot_weight.dtype),
+        )
     gradient_start = lax.axis_index("tensor") * gradient_slice
     gradient_listing = ([], [], [], [])
     input_rows = recv_x[0]
@@ -162,11 +181,16 @@
         lax.psum(stacked[2].astype(jnp.bfloat16), "dp").astype(jnp.float32),
         lax.psum(stacked[3].astype(jnp.bfloat16), "dp").astype(jnp.float32),
     )
-    returned = lax.all_to_all(
-        jnp.stack(dx_list, axis=0), "expert", split_axis=1, concat_axis=0, tiled=True
-    )
-    flat_rows = returned.reshape(slots_all, gradient_slice)
-    input_grad = contract_product(placing, flat_rows, 0, 0).astype(brain_float_half)
+    if dense:
+        input_grad = lax.psum_scatter(
+            dx_list[0], "expert", scatter_dimension=0, tiled=True
+        )
+    else:
+        returned = lax.all_to_all(
+            jnp.stack(dx_list, axis=0), "expert", split_axis=1, concat_axis=0, tiled=True
+        )
+        flat_rows = returned.reshape(slots_all, gradient_slice)
+        input_grad = contract_product(placing, flat_rows, 0, 0).astype(brain_float_half)
     return (
         input_grad,
         input_first_gradient,

time: 352 us -> 256 us (0.73)
  local copies, waits for them, and re-layouts: 53 us -> 8.58 us
  starting transfers between devices: 21.5 us -> 0.5 us
  other arithmetic: 24.6 us -> 6.44 us
  matrix products: 47.9 us -> 37.6 us
  waiting for transfers between devices: 167 us -> 159 us
  blocking collectives: 21.8 us -> 29.1 us
    all_to_all x4 -> x0, waiting for transfers between devices: 119 us -> none  [the longest x1 61.2 us: shards(): lax.all_to_all(sent_x, 'expert', split_axis=0, concat_axis=1, tiled=True)]
    all_gather x0 -> x4, waiting for transfers between devices: none -> 84 us  [the longest x1 39.7 us: shards(): half_x = lax.all_gather(activations, 'expert', axis=0, tiled=True)]
    unnamed x3 -> x9, waiting for transfers between devices: 0.05 us -> 34.3 us
    all_to_all x4 -> x0, starting transfers between devices: 21 us -> none  [the longest x1 6.32 us: shards(): lax.all_to_all(slot_weight.astype(jnp.bfloat16), 'expert', split_axis=0,...]
    convert_element_type x4 -> x0, local copies, waits for them, and re-layouts: 15.2 us -> none  [the longest x1 5.42 us: shards(): dy_rows.astype(single_float)]
    unnamed x4 -> x2, other arithmetic: 12.9 us -> 0.03 us
    dot_general x10 -> x9, matrix products: 26.1 us -> 16.3 us  [contract_product(): lax.dot_general(left, right, (((left_dim,), (right_dim,)), ((), ())), pre...]
    all_to_all x2 -> x0, local copies, waits for them, and re-layouts: 9.46 us -> none  [the longest x1 6.12 us: shards(): lax.all_to_all(jnp.stack(dx_list, axis=0), 'expert', split_axis=1, concat...]
  transfers between devices with their start and end apart: 7 -> 8, of which waited for: 5 -> 7; matrix products, arithmetic and copies ran while one was open for 13% -> 13% of each run, Pallas kernels for 0% -> 0%
where the time goes in v1:
time: 256 us
  waiting for transfers between devices  159 us (62%)
  matrix products  37.6 us (15%)
  blocking collectives  29.1 us (11%)
  between operations  14.4 us (6%)
  local copies, waits for them, and re-layouts  8.58 us (3%)
  other arithmetic  6.44 us (3%)
    all_gather x1, waiting for transfers between devices, shards(): half_x = lax.all_gather(activations, 'expert', axis=0, tiled=True)  39.7 us
    all_gather x1, waiting for transfers between devices, shards(): half_dy = lax.all_gather(output_gradient, 'expert', axis=0, tiled=True)  35.8 us
    unnamed x9, waiting for transfers between devices  34.3 us
    psum x1, waiting for transfers between devices, shards(): lax.psum(stacked[1].astype(jnp.bfloat16), 'dp').astype(jnp.float32)  26.7 us
    psum x1, blocking collectives, shards(): lax.psum(stacked[2].astype(jnp.bfloat16), 'dp').astype(jnp.float32)  17.2 us
    dot_general x9, matrix products, contract_product(): lax.dot_general(left, right, (((left_dim,), (right_dim,)), ((), ())), pre...  16.3 us
    all_gather x1, blocking collectives, shards(): weights = lax.all_gather(token_weight, 'expert', axis=0, tiled=True)  11.9 us
    dot_general x1, matrix products, shards(): jnp.einsum('rjf,jfd->rd', dz_scaled, gate_up_weight[0], preferred_element...  10.9 us
  transfers between devices with their start and end apart: 8, of which 7 were waited for; matrix products, arithmetic and copies ran while one was open for 13% of the time, Pallas kernels for 0%

profile of v1, /device:TPU:0, one launch (start us, length us, event | category | flops | bytes accessed | tf_op | source)
XLA Modules:
  0.0 255.7 jit_solution(7548520528369759734)
XLA Ops:
  7.2 0.0 copy-start
  7.2 0.0 all-gather.9.cloned.1.call-start
  7.2 0.7 all-gather.9.cloned.1.call-update
  7.9 0.0 all-gather.5.cloned.1.call-start
  8.0 0.7 all-gather.5.cloned.1.call-update
  8.7 0.0 all-gather.11.cloned.1.call-start
  8.7 39.7 %all-gather.9.cloned.1.call-done = bf16[512,1440]{0,1:T(8,128)(2,1)} async-done(((bf16[128,1440]{0,1:T(8,128)(2,1)}), bf16[512,1440]{0,1:T(8,128)(2,1)}) %all-gather.9.cloned.1.call-update) | async-done | bytes 1474576 | tf_op jit(solution)/shard_map/all_gather | solution.py:51
  48.4 0.0 all-gather.11.cloned.1.call-update
  48.5 0.0 all-gather.7.cloned.1.call-start
  48.5 35.8 %all-gather.5.cloned.1.call-done = bf16[512,1440]{0,1:T(8,128)(2,1)} async-done(((bf16[128,1440]{0,1:T(8,128)(2,1)}), bf16[512,1440]{0,1:T(8,128)(2,1)}) %all-gather.5.cloned.1.call-update) | async-done | bytes 1474576 | tf_op jit(solution)/shard_map/all_gather | solution.py:52
  84.4 0.0 all-gather.7.cloned.1.call-update
  84.4 0.0 all-reduce.7.cloned.1.call-start
  84.6 11.9 %all_gather.15 = f32[512,4]{0,1:T(4,128)S(1)} all-gather(f32[128,4]{0,1:T(4,128)S(1)} %select_reduce_fusion), channel_id=1, replica_groups=mesh['dp'=4,'expert'=4,'tensor'=2] {'expert'}, dimensions={0}, use_global_device_ids=true | all-gather | bytes 10240 | tf_op jit(solution)/shard_map/all_gather | solution.py:53
  96.5 0.0 all-gather.11.cloned.1.call-done
  96.5 2.4 convolution_convert_fusion.1
  98.9 1.5 fusion.39
  100.5 1.6 fusion.40
  102.1 8.4 %all-gather.7.cloned.1.call-done = bf16[512,2880]{0,1:T(8,128)(2,1)} async-done(((bf16[512,1440]{0,1:T(8,128)(2,1)}), bf16[512,2880]{0,1:T(8,128)(2,1)}) %all-gather.7.cloned.1.call-update) | async-done | bytes 2949136 | tf_op jit(solution)/shard_map/all_gather | solution.py:57
  110.5 2.6 %multiply_convert_fusion.1 = bf16[512,2880]{0,1:T(8,128)(2,1)S(1)} fusion(bf16[512,2880]{0,1:T(8,128)(2,1)} %all-gather.7.cloned.1.call-done, f32[512]{0:T(512)S(1)} %bitcast.83), kind=kLoop, calls=%fused_computation.4 | loop fusion | flops 4423680 | bytes 5900288 | tf_op jit(solution)/shard_map/convert_element_type | solution.py:98
  113.1 0.0 slice-start.1
  113.1 0.6 convolution_convert_fusion.2
  113.7 0.0 copy-start.1
  113.7 0.0 copy-start.7
  113.7 0.0 slice-start.2
  113.7 2.6 %fusion.8 = f32[512,720]{0,1:T(8,128)S(1)} fusion(bf16[1,720,2880]{2,1,0:T(8,128)(2,1)S(1)} %copy-done.16, bf16[512,2880]{0,1:T(8,128)(2,1)S(1)} %multiply_convert_fusion.1, f32[2880]{0:T(1024)S(1)} %reduce), kind=kOutput, calls=%fused_computation.9 | convolution fusion | flops 2127790080 | bytes 8582400 | tf_op jit(solution)/shard_map/dot_general | solution.py:11
  116.3 0.0 slice-done.1
  116.3 0.8 copy-done.1
  117.2 0.4 copy-done.7
  117.5 2.4 multiply_add_fusion
  120.0 0.0 copy-done.6
  120.0 0.0 copy-start.11
  120.0 2.4 add_add_fusion
  122.5 0.0 copy-done.11
  122.5 1.2 multiply_convert_fusion.5
  123.7 0.0 copy-start.4
  123.7 0.9 copy-done.4
  124.6 0.9 convolution_convert_fusion
  125.5 0.0 copy-done.3
  125.6 0.9 fusion.31
  126.5 0.0 all-reduce.7.cloned.1.call-update
  126.5 0.2 reduce-scatter.5.cloned.1.call-start
  126.8 10.9 %bitcast_convert_fusion = bf16[512,2880]{0,1:T(8,128)(2,1)} fusion(bf16[1,2,720,2880]{3,2,1,0:T(8,128)(2,1)} %param.16, f32[512,1,720]{0,2,1:T(8,128)} %copy-done.3, f32[512,1,720]{0,2,1:T(8,128)} %copy-done.2, f32[2,720]{1,0:T(2,128)S(1)} %bitcast.84), kind=kOutput, calls=%fused_computation.2 | convolution fusion | flops 4250419200 | bytes 14198400 | tf_op jit(solution)/shard_map/rjf,jfd->rd/dot_general | solution.py:146
  137.7 0.0 reduce-scatter.5.cloned.1.call-update
  137.7 0.0 all-reduce.5.cloned.1.call-start
  137.8 3.0 %fusion.29 = bf16[1,32,2,720]{3,1,2,0:T(8,128)(2,1)} fusion(f32[512,1,720]{0,2,1:T(8,128)} %copy-done.3, f32[512,1,720]{0,2,1:T(8,128)} %copy-done.2, bf16[512,32]{0,1:T(8,128)(2,1)S(1)} %convolution_convert_fusion.1), kind=kOutput, calls=%fused_computation.39 | convolution fusion | flops 50227200 | bytes 3074048 | tf_op jit(solution)/shard_map/hp,hwl->pwl/dot_general | solution.py:164
  140.8 4.9 %all-reduce.7.cloned.1.call-done = (bf16[512,32]{0,1:T(8,128)(2,1)}, bf16[512,32]{0,1:T(8,128)(2,1)}) async-done(((bf16[512,32]{0,1:T(8,128)(2,1)}, bf16[512,32]{0,1:T(8,128)(2,1)}), (bf16[512,32]{0,1:T(8,128)(2,1)}, bf16[512,32]{0,1:T(8,128)(2,1)})) %all-reduce.7.cloned.1.call-update) | async-done | bytes 65552 | tf_op jit(solution)/shard_map/psum | solution.py:143
  145.6 2.0 fusion.18
  147.6 2.6 %fusion.19 = bf16[1,1440,32]{1,2,0:T(8,128)(2,1)} fusion(bf16[512,32]{0,1:T(8,128)(2,1)S(1)} %copy-done.10, bf16[512,2880]{0,1:T(8,128)(2,1)} %all-gather.11.cloned.1.call-done, s32[]{:T(128)S(6)} %select_n.14), kind=kOutput, calls=%fused_computation.25 | convolution fusion | flops 47278080 | bytes 1599492 | tf_op jit(solution)/shard_map/dot_general | solution.py:11
  150.2 0.0 all-reduce.5.cloned.1.call-update
  150.2 0.0 reduce-scatter.7.cloned.1.call-start
  150.3 9.3 %reduce-scatter.5.cloned.1.call-done = bf16[512,1440]{0,1:T(8,128)(2,1)} async-done(((bf16[512,2880]{0,1:T(8,128)(2,1)}), bf16[512,1440]{0,1:T(8,128)(2,1)}) %reduce-scatter.5.cloned.1.call-update) | async-done | bytes 1474576 | tf_op jit(solution)/shard_map/reduce_scatter | solution.py:149
  159.5 2.1 fusion.13
  161.7 1.6 copy.31
  163.3 0.0 reduce-scatter.7.cloned.1.call-update
  163.3 1.1 copy-done.5
  164.4 0.3 fusion.32
  164.8 17.2 %psum.45 = bf16[1,720,32]{1,2,0:T(8,128)(2,1)S(1)} all-reduce(bf16[1,720,32]{1,2,0:T(8,128)(2,1)S(1)} %fusion.32), channel_id=1, replica_groups=mesh['dp'=4,'expert'=4,'tensor'=2] {'dp'}, use_global_device_ids=true, to_apply=%region_6.7 | all-reduce | flops 23040 | bytes 92160 | tf_op jit(solution)/shard_map/psum | solution.py:181
  182.0 0.6 convert_element_type.103
  182.7 26.7 %all-reduce.5.cloned.1.call-done = (bf16[1,32,2,720]{3,1,2,0:T(8,128)(2,1)}, bf16[1,1440,32]{1,2,0:T(8,128)(2,1)}, bf16[1,32,1440]{2,1,0:T(8,128)(2,1)}) async-done(((bf16[1,32,2,720]{3,1,2,0:T(8,128)(2,1)}, bf16[1,1440,32]{1,2,0:T(8,128)(2,1)}, bf16[1,32,1440]{2,1,0:T(8,128)(2,1)}), (bf16[1,32,2,720]{3,1,2,0:T(8,128)(2,1)}, bf16[1,1440,32]{1,2,0:T(8,128)(2,1)}, ...) | async-done | bytes 276496 | tf_op jit(solution)/shard_map/psum | solution.py:180
  209.3 1.7 copy.30
  211.0 1.6 convert_element_type.96
  212.6 1.6 convert_element_type.107
  214.1 32.8 %reduce-scatter.7.cloned.1.call-done = bf16[128,1440]{1,0:T(8,128)(2,1)} async-done(((bf16[512,1440]{1,0:T(8,128)(2,1)}), bf16[128,1440]{1,0:T(8,128)(2,1)}) %reduce-scatter.7.cloned.1.call-update) | async-done | bytes 368656
  246.9 1.9 copy.32
  (31 shorter events, 0.1 us)
Async XLA Ops:
  7.2 89.3 %copy-start = (bf16[1,2880,32]{1,2,0:T(8,128)(2,1)S(1)}, bf16[1,2880,32]{1,2,0:T(8,128)(2,1)}, u32[]{:S(2)}) copy-start(bf16[1,2880,32]{1,2,0:T(8,128)(2,1)} %param.20) | copy-start | bytes 552964
  7.2 41.2 %all-gather.9.cloned.1.call-start = ((), (), s32[]{:S(2)}) async-start(), calls=%async_computation.4 | async-start | bytes 1843200 | tf_op jit(solution)/shard_map/all_gather | solution.py:51
  7.9 76.4 %all-gather.5.cloned.1.call-start = ((), (), s32[]{:S(2)}) async-start(), calls=%async_computation.2 | async-start | bytes 1843200 | tf_op jit(solution)/shard_map/all_gather | solution.py:52
  8.7 87.8 %all-gather.11.cloned.1.call-start = ((), (), s32[]{:S(2)}) async-start(), calls=%async_computation.5 | async-start | bytes 4423680 | tf_op jit(solution)/shard_map/all_gather | solution.py:56
  48.4 36.0 %copy-start.8 = (bf16[1,32,2,720]{3,2,1,0:T(2,128)(2,1)S(1)}, bf16[1,32,2,720]{3,2,1,0:T(2,128)(2,1)}, u32[]{:S(2)}) copy-start(bf16[1,32,2,720]{3,2,1,0:T(2,128)(2,1)} %param.21) | copy-start | bytes 276484
  48.4 36.0 %copy-start.12 = (f32[1,2880]{1,0:T(1,128)S(1)}, f32[1,2880]{1,0:T(1,128)}, u32[]{:S(2)}) copy-start(f32[1,2880]{1,0:T(1,128)} %param.19) | copy-start | bytes 34564
  48.4 36.1 %copy-start.14 = (f32[128,4]{0,1:T(4,128)S(1)}, f32[128,4]{0,1:T(4,128)}, u32[]{:S(2)}) copy-start(f32[128,4]{0,1:T(4,128)} %param.14) | copy-start | bytes 6148
  48.4 36.1 %copy-start.15 = (s32[128,4]{0,1:T(4,128)S(1)}, s32[128,4]{0,1:T(4,128)}, u32[]{:S(2)}) copy-start(s32[128,4]{0,1:T(4,128)} %param.15) | copy-start | bytes 6148
  48.4 48.0 %copy-start.13 = (f32[1,2,720]{2,1,0:T(2,128)S(1)}, f32[1,2,720]{2,1,0:T(2,128)}, u32[]{:S(2)}) copy-start(f32[1,2,720]{2,1,0:T(2,128)} %param.17) | copy-start | bytes 17284
  48.5 62.0 %all-gather.7.cloned.1.call-start = ((), (), s32[]{:S(2)}) async-start(), calls=%async_computation.3 | async-start | bytes 4423680 | tf_op jit(solution)/shard_map/all_gather | solution.py:57
  84.4 61.3 %all-reduce.7.cloned.1.call-start = ((), (), s32[]{:S(2)}) async-start(), calls=%async_computation.9 | async-start | bytes 131072 | tf_op jit(solution)/shard_map/psum | solution.py:143
  110.4 2.6 %copy-start.9 = (bf16[1,32,2880]{2,1,0:T(8,128)(2,1)S(1)}, bf16[1,32,2880]{2,1,0:T(8,128)(2,1)}, u32[]{:S(2)}) copy-start(bf16[1,32,2880]{2,1,0:T(8,128)(2,1)} %param.23) | copy-start | bytes 552964
  110.5 3.2 %copy-start.16 = (bf16[1,720,2880]{2,1,0:T(8,128)(2,1)S(1)}, bf16[1,720,2880]{2,1,0:T(8,128)(2,1)}, u32[]{:S(2)}) copy-start(bf16[1,720,2880]{2,1,0:T(8,128)(2,1)} %param.18) | copy-start | bytes 12441604
  110.5 5.8 %slice-start = ((s8[8478720]{0:T(1024)(128)(4,1)}), s8[4194304]{0:T(1024)(128)(4,1)S(1)}, s32[]{:S(2)}) async-start(s8[8478720]{0:T(1024)(128)(4,1)} %bitcast.85), calls=%async_computation.10 | async-start | bytes 8388608
  113.1 3.3 %slice-start.1 = ((s8[8478720]{0:T(1024)(128)(4,1)}), s8[4194304]{0:T(1024)(128)(4,1)S(1)}, s32[]{:S(2)}) async-start(s8[8478720]{0:T(1024)(128)(4,1)} %bitcast.85), calls=%async_computation.11 | async-start | bytes 8388608
  113.7 3.5 %copy-start.1 = (bf16[512,2880]{0,1:T(8,128)(2,1)S(1)}, bf16[512,2880]{0,1:T(8,128)(2,1)}, u32[]{:S(2)}) copy-start(bf16[512,2880]{0,1:T(8,128)(2,1)} %all-gather.11.cloned.1.call-done) | copy-start | bytes 8847364
  113.7 3.8 %copy-start.7 = (f32[512,720]{0,1:T(8,128)S(1)}, f32[512,720]{0,1:T(8,128)}, u32[]{:S(2)}) copy-start(f32[512,720]{0,1:T(8,128)} %fusion.39) | copy-start | bytes 4423684
  113.7 3.8 %slice-start.2 = ((s8[8478720]{0:T(1024)(128)(4,1)}), s8[90112]{0:T(1024)(128)(4,1)S(1)}, s32[]{:S(2)}) async-start(s8[8478720]{0:T(1024)(128)(4,1)} %bitcast.85), calls=%async_computation.12 | async-start | bytes 180224
  117.5 2.4 copy-start.6
  120.0 2.5 copy-start.11
  123.7 0.9 copy-start.4
  123.7 1.8 copy-start.2
  123.7 1.8 copy-start.3
  126.5 33.0 %reduce-scatter.5.cloned.1.call-start = ((), (), s32[]{:S(2)}) async-start(), calls=%async_computation.6 | async-start | bytes 4423680 | tf_op jit(solution)/shard_map/reduce_scatter | solution.py:149
  137.7 71.6 %all-reduce.5.cloned.1.call-start = ((), (), s32[]{:S(2)}) async-start(), calls=%async_computation.8 | async-start | bytes 589824 | tf_op jit(solution)/shard_map/psum | solution.py:180
  145.6 2.0 copy-start.10
  150.2 96.7 %reduce-scatter.7.cloned.1.call-start = ((), (), s32[]{:S(2)}) async-start(), calls=%async_computation.7 | async-start | bytes 1966080
  163.3 1.1 copy-start.5
Sparse Core Ops, SparseCore 0:
  9.6 38.8 all-gather.8
  50.0 34.3 all-gather.4
  85.9 10.0 all-gather.10
  97.4 12.9 all-gather.6
  126.7 18.9 all-reduce.6
  147.8 11.7 reduce-scatter.4
  163.6 45.6 all-reduce.4
  211.6 35.2 reduce-scatter.6

commit v2 on v1

--- a/solution.py
+++ b/solution.py
@@ -1,6 +1,10 @@
+import functools
+
 import jax
 import jax.numpy as jnp
 from jax import lax
+from jax.experimental import pallas as pl
+from jax.experimental.pallas import tpu as pltpu
 from jax.sharding import PartitionSpec as P
 
 ALPHA = 1.702
@@ -11,6 +15,305 @@
     return lax.dot_general(
         left, right, (((left_dim,), (right_dim,)), ((), ())), preferred_element_type=jnp.float32
     )
+
+
+MESH = pl.DeviceIdType.MESH
+
+
+def remote(src, dst, send, recv, **where):
+    return pltpu.make_async_remote_copy(
+        src_ref=src, dst_ref=dst, send_sem=send, recv_sem=recv, device_id=where, device_id_type=MESH
+    )
+
+
+def gather_kernel(
+    n, x_ref, dy_ref, w_ref, x_out, dy_out, w_out, held,
+    line_send, line_recv, pair_send, pair_recv, w_send, w_recv,
+):
+    e = lax.axis_index("expert")
+    c = lax.axis_index("tensor")
+    rows, width = x_ref.shape
+    barrier = pltpu.get_barrier_semaphore()
+    for j in range(1, n):
+        pl.semaphore_signal(
+            barrier, inc=1, device_id={"expert": lax.rem(e + j, n)}, device_id_type=MESH
+        )
+    pl.semaphore_signal(barrier, inc=1, device_id={"tensor": 1 - c}, device_id_type=MESH)
+    pl.semaphore_wait(barrier, n)
+
+    def piece(a, s):
+        return held.at[a, s, c]
+
+    def block(direction, k):
+        return e - k if direction == 0 else e + k
+
+    def arrives(direction, k):
+        return e >= k if direction == 0 else e + k <= n - 1
+
+    def goes_on(direction):
+        return e < n - 1 if direction == 0 else e > 0
+
+    def line(a, direction, k):
+        s = block(direction, k)
+        return remote(
+            piece(a, s), piece(a, s), line_send.at[a, direction, k], line_recv.at[a, direction, k],
+            expert=e + 1 if direction == 0 else e - 1,
+        )
+
+    def line_in(a, direction, k):
+        s = block(direction, k)
+        return remote(
+            piece(a, s), piece(a, s),
+            line_send.at[a, direction, k - 1], line_recv.at[a, direction, k - 1],
+            expert=e - 1 if direction == 0 else e + 1,
+        )
+
+    def pair(a, s, slot):
+        return remote(
+            piece(a, s), piece(a, s), pair_send.at[a, slot], pair_recv.at[a, slot], tensor=1 - c
+        )
+
+    def pair_in(a, s, slot):
+        other = held.at[a, s, 1 - c]
+        return remote(other, other, pair_send.at[a, slot], pair_recv.at[a, slot], tensor=1 - c)
+
+    def own(a):
+        for direction in range(2):
+            @pl.when(goes_on(direction))
+            def _():
+                line(a, direction, 0).start()
+        pair(a, e, 0).start()
+
+    def hop(a, k):
+        for direction in range(2):
+            @pl.when(arrives(direction, k))
+            def _():
+                line_in(a, direction, k).wait_recv()
+                if k < n - 1:
+                    @pl.when(goes_on(direction))
+                    def _():
+                        line(a, direction, k).start()
+                pair(a, block(direction, k), direction * (n - 1) + k).start()
+
+    def settle(a, out):
+        def lay(s):
+            where = pl.ds(pl.multiple_of(s * rows, rows), rows)
+            out[where, :] = jnp.concatenate([held[a, s, 0], held[a, s, 1]], axis=1)
+
+        pair_in(a, e, 0).wait_recv()
+        lay(e)
+        for k in range(1, n):
+            for direction in range(2):
+                @pl.when(arrives(direction, k))
+                def _():
+                    s = block(direction, k)
+                    pair_in(a, s, direction * (n - 1) + k).wait_recv()
+                    lay(s)
+
+    held[0, e, c] = x_ref[...]
+    own(0)
+    held[1, e, c] = dy_ref[...]
+    for j in range(1, n):
+        remote(
+            w_ref, w_out.at[e], w_send.at[j], w_recv.at[j], expert=lax.rem(e + j, n)
+        ).start()
+    w_out[e] = w_ref[...]
+    hop(0, 1)
+    own(1)
+    for k in range(2, n):
+        hop(0, k)
+    hop(1, 1)
+    settle(0, x_out)
+    for k in range(2, n):
+        hop(1, k)
+    settle(1, dy_out)
+    for j in range(1, n):
+        source = lax.rem(e + n - j, n)
+        remote(
+            w_ref, w_out.at[source], w_send.at[j], w_recv.at[j], expert=source
+        ).wait()
+    for a in range(2):
+        pair(a, e, 0).wait_send()
+        for direction in range(2):
+            @pl.when(goes_on(direction))
+            def _():
+                line(a, direction, 0).wait_send()
+            for k in range(1, n):
+                @pl.when(arrives(direction, k))
+                def _():
+                    if k < n - 1:
+                        @pl.when(goes_on(direction))
+                        def _():
+                            line(a, direction, k).wait_send()
+                    pair(a, block(direction, k), direction * (n - 1) + k).wait_send()
+
+
+def gather_rows(x, dy, w):
+    n = lax.axis_size("expert")
+    cores = lax.axis_size("tensor")
+    rows, width = x.shape
+    whole = jax.ShapeDtypeStruct((n * rows, cores * width), x.dtype)
+    return pl.pallas_call(
+        functools.partial(gather_kernel, n),
+        out_shape=(whole, whole, jax.ShapeDtypeStruct((n,) + w.shape, w.dtype)),
+        in_specs=[pl.BlockSpec(memory_space=pltpu.VMEM)] * 3,
+        out_specs=[pl.BlockSpec(memory_space=pltpu.VMEM)] * 3,
+        scratch_shapes=[
+            pltpu.VMEM((2, n, cores, rows, width), x.dtype),
+            pltpu.SemaphoreType.DMA((2, 2, n)),
+            pltpu.SemaphoreType.DMA((2, 2, n)),
+            pltpu.SemaphoreType.DMA((2, 2 * n)),
+            pltpu.SemaphoreType.DMA((2, 2 * n)),
+            pltpu.SemaphoreType.DMA((n,)),
+            pltpu.SemaphoreType.DMA((n,)),
+        ],
+        compiler_params=pltpu.CompilerParams(
+            collective_id=0, has_side_effects=True, vmem_limit_bytes=32 * 2**20
+        ),
+    )(x, dy, w)
+
+
+def return_kernel(
+    n, m, rows_ref, wide_ref, thin_ref, out_ref, wide_out, thin_out,
+    from_up, from_down, summed, wide_in, thin_in,
+    line_send, line_recv, peer_send, peer_recv,
+):
+    e = lax.axis_index("expert")
+    d = lax.axis_index("dp")
+    wide_type = jnp.float32
+    barrier = pltpu.get_barrier_semaphore()
+    for j in range(1, n):
+        pl.semaphore_signal(
+            barrier, inc=1, device_id={"expert": lax.rem(e + j, n)}, device_id_type=MESH
+        )
+    for j in range(1, m):
+        pl.semaphore_signal(
+            barrier, inc=1, device_id={"dp": lax.rem(d + j, m)}, device_id_type=MESH
+        )
+    pl.semaphore_wait(barrier, n + m - 2)
+
+    landing = (from_up, from_down)
+
+    def outgoing(direction, t, src):
+        return remote(
+            src, landing[direction].at[t], line_send.at[t], line_recv.at[direction, t],
+            expert=e - 1 if direction == 0 else e + 1,
+        )
+
+    def incoming(direction, t):
+        dst = landing[direction].at[t]
+        return remote(
+            dst, dst, line_send.at[t], line_recv.at[direction, t],
+            expert=e + 1 if direction == 0 else e - 1,
+        )
+
+    def target(direction, step):
+        return step - (n - 1) + e if direction == 0 else n - 1 - step + e
+
+    def sends(direction, step):
+        t = target(direction, step)
+        if direction == 0:
+            return jnp.logical_and(t >= 0, t < e)
+        return jnp.logical_and(t <= n - 1, t > e)
+
+    def starts_line(direction):
+        return e == n - 1 if direction == 0 else e == 0
+
+    def line_step(step):
+        for direction in range(2):
+            t = target(direction, step)
+            go = sends(direction, step)
+
+            @pl.when(jnp.logical_and(go, starts_line(direction)))
+            def _():
+                outgoing(direction, t, rows_ref.at[t]).start()
+
+            @pl.when(jnp.logical_and(go, jnp.logical_not(starts_line(direction))))
+            def _():
+                incoming(direction, t).wait_recv()
+                summed[t] = (
+                    landing[direction][t].astype(wide_type) + rows_ref[t].astype(wide_type)
+                ).astype(summed.dtype)
+                outgoing(direction, t, summed.at[t]).start()
+
+    line_step(0)
+    pieces = ((wide_ref, wide_in), (thin_ref, thin_in))
+    for j in range(1, m):
+        for i, (src, dst) in enumerate(pieces):
+            remote(
+                src, dst.at[j - 1], peer_send.at[i, j], peer_recv.at[i, j], dp=lax.rem(d + j, m)
+            ).start()
+    for step in range(1, n - 1):
+        line_step(step)
+    for i, ((src, dst), out) in enumerate(zip(pieces, (wide_out, thin_out))):
+        total = src[...].astype(wide_type)
+        for j in range(1, m):
+            remote(
+                src, dst.at[j - 1], peer_send.at[i, j], peer_recv.at[i, j], dp=lax.rem(d + j, m)
+            ).wait()
+            total = total + dst[j - 1].astype(wide_type)
+        out[...] = total
+
+    @pl.when(e == 0)
+    def _():
+        incoming(0, e).wait_recv()
+        out_ref[...] = (rows_ref[e].astype(wide_type) + from_up[e].astype(wide_type)).astype(
+            out_ref.dtype
+        )
+
+    @pl.when(e == n - 1)
+    def _():
+        incoming(1, e).wait_recv()
+        out_ref[...] = (rows_ref[e].astype(wide_type) + from_down[e].astype(wide_type)).astype(
+            out_ref.dtype
+        )
+
+    @pl.when(jnp.logical_and(e > 0, e < n - 1))
+    def _():
+        incoming(0, e).wait_recv()
+        incoming(1, e).wait_recv()
+        out_ref[...] = (
+            rows_ref[e].astype(wide_type)
+            + from_up[e].astype(wide_type)
+            + from_down[e].astype(wide_type)
+        ).astype(out_ref.dtype)
+
+    for step in range(n - 1):
+        for direction in range(2):
+            @pl.when(sends(direction, step))
+            def _():
+                t = target(direction, step)
+                outgoing(direction, t, summed.at[t]).wait_send()
+
+
+def return_rows(dx, wide, thin):
+    n = lax.axis_size("expert")
+    m = lax.axis_size("dp")
+    shape = (n, dx.shape[0] // n, dx.shape[1])
+    return pl.pallas_call(
+        functools.partial(return_kernel, n, m),
+        out_shape=(
+            jax.ShapeDtypeStruct(shape[1:], dx.dtype),
+            jax.ShapeDtypeStruct(wide.shape, jnp.float32),
+            jax.ShapeDtypeStruct(thin.shape, jnp.float32),
+        ),
+        in_specs=[pl.BlockSpec(memory_space=pltpu.VMEM)] * 3,
+        out_specs=[pl.BlockSpec(memory_space=pltpu.VMEM)] * 3,
+        scratch_shapes=[
+            pltpu.VMEM(shape, dx.dtype),
+            pltpu.VMEM(shape, dx.dtype),
+            pltpu.VMEM(shape, dx.dtype),
+            pltpu.VMEM((m - 1,) + wide.shape, wide.dtype),
+            pltpu.VMEM((m - 1,) + thin.shape, thin.dtype),
+            pltpu.SemaphoreType.DMA((n,)),
+            pltpu.SemaphoreType.DMA((2, n)),
+            pltpu.SemaphoreType.DMA((2, m)),
+            pltpu.SemaphoreType.DMA((2, m)),
+        ],
+        compiler_params=pltpu.CompilerParams(
+            collective_id=1, has_side_effects=True, vmem_limit_bytes=32 * 2**20
+        ),
+    )(dx.reshape(shape), wide, thin)
 
 
 def shards(
@@ -37,7 +340,12 @@
     capacity = min(tok_rows * top_count * 11 // (8 * experts_all), tok_rows)
     gradient_slice = activations.shape[1]
     slots_all = experts_all * capacity
-    dense = experts_all == top_count and capacity == tok_rows
+    dense = (
+        experts_all == top_count
+        and capacity == tok_rows
+        and local_count == 1
+        and lax.axis_size("tensor") == 2
+    )
     if dense:
         expert_ids = jnp.arange(experts_all, dtype=jnp.int32)
         token_weight = jnp.sum(
@@ -48,13 +356,12 @@
             ),
             axis=1,
         )
-        half_x = lax.all_gather(activations, "expert", axis=0, tiled=True)
-        half_dy = lax.all_gather(output_gradient, "expert", axis=0, tiled=True)
-        weights = lax.all_gather(token_weight, "expert", axis=0, tiled=True)
+        spread = jnp.zeros((-(-experts_all // 8) * 8, tok_rows), jnp.float32)
+        spread = lax.dynamic_update_slice(spread, token_weight.T, (0, 0))
+        rows_x, rows_dy, weights = gather_rows(activations, output_gradient, spread)
         mine = lax.axis_index("expert")
         recv_w = lax.dynamic_slice_in_dim(weights, mine, 1, 1).reshape(1, -1)
-        recv_x = lax.all_gather(half_x, "tensor", axis=1, tiled=True)[None]
-        recv_dy = lax.all_gather(half_dy, "tensor", axis=1, tiled=True)[None]
+        recv_x, recv_dy = rows_x[None], rows_dy[None]
     else:
         flat_experts = token_experts.reshape(tok_rows * top_count)
         onehot = (flat_experts[:, None] == jnp.arange(experts_all, dtype=jnp.int32)[None, :]).astype(
@@ -158,6 +465,36 @@
     dx_list = [input_gradient_rows]
     input_columns = lax.dynamic_slice_in_dim(input_rows, gradient_start, gradient_slice, 1)
     gradient_columns = lax.dynamic_slice_in_dim(gradient_rows, gradient_start, gradient_slice, 1)
+    if dense:
+        rank = input_adapter.shape[1]
+        hidden_count = hidden_units.shape[1]
+        wide = jnp.concatenate(
+            [
+                contract_product(input_adapter, input_columns, 0, 0),
+                contract_product(down_adapter, gradient_columns, 0, 0),
+            ],
+            axis=0,
+        )
+        thin = jnp.concatenate(
+            [
+                contract_product(adapter_input_rows, adapter_mid_gradient[:, 0], 0, 0),
+                contract_product(adapter_input_rows, adapter_mid_gradient[:, 1], 0, 0),
+                contract_product(backward_adapter, hidden_units, 0, 0),
+            ],
+            axis=0,
+        )
+        input_grad, wide_sum, thin_sum = return_rows(
+            dx_list[0],
+            (ADAPTER_SCALE * wide).astype(brain_float_half),
+            (ADAPTER_SCALE * thin).astype(brain_float_half),
+        )
+        return (
+            input_grad,
+            wide_sum[:rank].T[None],
+            jnp.stack([thin_sum[:rank], thin_sum[rank : 2 * rank]], axis=1)[None],
+            thin_sum[2 * rank :].T[None],
+            wide_sum[rank:][None],
+        )
     gradient_listing[0].append(ADAPTER_SCALE * contract_product(input_columns, input_adapter, 0, 0))
     gradient_listing[1].append(
         ADAPTER_SCALE
@@ -181,16 +518,11 @@
         lax.psum(stacked[2].astype(jnp.bfloat16), "dp").astype(jnp.float32),
         lax.psum(stacked[3].astype(jnp.bfloat16), "dp").astype(jnp.float32),
     )
-    if dense:
-        input_grad = lax.psum_scatter(
-            dx_list[0], "expert", scatter_dimension=0, tiled=True
-        )
-    else:
-        returned = lax.all_to_all(
-            jnp.stack(dx_list, axis=0), "expert", split_axis=1, concat_axis=0, tiled=True
-        )
-        flat_rows = returned.reshape(slots_all, gradient_slice)
-        input_grad = contract_product(placing, flat_rows, 0, 0).astype(brain_float_half)
+    returned = lax.all_to_all(
+        jnp.stack(dx_list, axis=0), "expert", split_axis=1, concat_axis=0, tiled=True
+    )
+    flat_rows = returned.reshape(slots_all, gradient_slice)
+    input_grad = contract_product(placing, flat_rows, 0, 0).astype(brain_float_half)
     return (
         input_grad,
         input_first_gradient,

time: 256 us -> 182 us (0.71)
  waiting for transfers between devices: 159 us -> 13.3 us
  Pallas kernels: 0 us -> 92.8 us
  blocking collectives: 29.1 us -> 0 us
  local copies, waits for them, and re-layouts: 8.58 us -> 15.5 us
  matrix products: 37.6 us -> 42 us
  other arithmetic: 6.44 us -> 3.08 us
    pallas_call x0 -> x2, Pallas kernels: none -> 92.8 us  [the longest x1 59.9 us: gather_rows(): pl.pallas_call(functools.partial(gather_kernel, n), out_shape=(whole, who...]
    all_gather x4 -> x0, waiting for transfers between devices: 84 us -> none  [the longest x1 39.7 us: shards(): half_x = lax.all_gather(activations, 'expert', axis=0, tiled=True)]
    unnamed x9 -> x2, waiting for transfers between devices: 34.3 us -> 0.03 us
    psum x1 -> x0, waiting for transfers between devices: 26.7 us -> none  [shards(): lax.psum(stacked[1].astype(jnp.bfloat16), 'dp').astype(jnp.float32)]
    psum x1 -> x0, blocking collectives: 17.2 us -> none  [shards(): lax.psum(stacked[2].astype(jnp.bfloat16), 'dp').astype(jnp.float32)]
    all_gather x1 -> x0, blocking collectives: 11.9 us -> none  [shards(): weights = lax.all_gather(token_weight, 'expert', axis=0, tiled=True)]
    dot_general x9 -> x11, matrix products: 16.3 us -> 25.3 us  [contract_product(): lax.dot_general(left, right, (((left_dim,), (right_dim,)), ((), ())), pre...]
    unnamed x44 -> x53, local copies, waits for them, and re-layouts: 8.55 us -> 12.4 us
  transfers between devices with their start and end apart: 8 -> 2, of which waited for: 7 -> 2; matrix products, arithmetic and copies ran while one was open for 13% -> 10% of each run, Pallas kernels for 0% -> 0%
where the time goes in v2:
time: 182 us; the launch traced here: 181 us
  Pallas kernels  92.8 us (51%)
  matrix products  42 us (23%)
  local copies, waits for them, and re-layouts  15.5 us (9%)
  between operations  14.4 us (8%)
  waiting for transfers between devices  13.3 us (7%)
  other arithmetic  3.08 us (2%)
    pallas_call x1, Pallas kernels, gather_rows(): pl.pallas_call(functools.partial(gather_kernel, n), out_shape=(whole, who...  59.9 us
    pallas_call x1, Pallas kernels, return_rows(): pl.pallas_call(functools.partial(return_kernel, n, m), out_shape=(jax.Sha...  32.9 us
    dot_general x11, matrix products, contract_product(): lax.dot_general(left, right, (((left_dim,), (right_dim,)), ((), ())), pre...  25.3 us
    unnamed x53, local copies, waits for them, and re-layouts  12.4 us
    dot_general x1, matrix products, shards(): jnp.einsum('rjf,jfd->rd', dz_scaled, gate_up_weight[0], preferred_element...  10.9 us
    reduce_scatter x1, waiting for transfers between devices, shards(): lax.psum_scatter(partial_value.astype(jnp.bfloat16), 'tensor', scatter_di...  10.5 us
  transfers between devices with their start and end apart: 2, of which 2 were waited for; matrix products, arithmetic and copies ran while one was open for 10% of the time, Pallas kernels for 0%

profile of v2, /device:TPU:0, one launch (start us, length us, event | category | flops | bytes accessed | tf_op | source)
XLA Modules:
  0.0 181.4 jit_solution(11712235121932435680)
XLA Ops:
  7.2 0.0 copy-start
  7.2 0.0 copy-start.12
  7.2 0.0 copy-start.19
  7.2 0.0 copy-start.20
  7.2 0.0 all-reduce.4.cloned.1.call-start
  7.3 1.9 %copy.33.x_ref = bf16[128,1440]{1,0:T(8,128)(2,1)} copy(bf16[128,1440]{0,1:T(8,128)(2,1)} %param.12) | data formatting | bytes 737280 | tf_op args[0]
  9.2 1.9 %copy.34.dy_ref = bf16[128,1440]{1,0:T(8,128)(2,1)} copy(bf16[128,1440]{0,1:T(8,128)(2,1)} %param.13) | data formatting | bytes 737280 | tf_op args[1]
  11.1 0.0 copy-done.12
  11.1 0.0 copy-done.19
  11.1 0.0 copy-done.20
  11.2 0.0 copy-start.2
  11.2 1.0 copy-done.2
  12.2 1.0 copy-done.3
  13.2 59.9 %shard_map.155 = (bf16[512,2880]{1,0:T(8,128)(2,1)S(1)}, bf16[512,2880]{1,0:T(8,128)(2,1)S(1)}, f32[4,8,128]{2,1,0:T(8,128)S(1)}) custom-call(bf16[128,1440]{1,0:T(8,128)(2,1)S(1)} %copy-done.2, bf16[128,1440]{1,0:T(8,128)(2,1)S(1)} %copy-done.3, f32[8,128]{1,0:T(8,128)S(1)} %dynamic_update_slice.3.w_ref), custom_call_target="tpu_custom_call" | custom-call | tf_op jit(solution)/shard_map/pallas_call | solution.py:156
  73.1 1.0 convolution_convert_fusion.1
  74.0 0.6 copy-done.1
  74.7 1.5 fusion.35
  76.2 1.5 fusion.36
  77.8 0.0 copy-start.13
  77.8 2.7 %multiply_convert_fusion.1 = bf16[512,2880]{1,0:T(8,128)(2,1)S(1)} fusion(bf16[512,2880]{1,0:T(8,128)(2,1)} %copy-done.1, f32[512]{0:T(512)S(1)} %bitcast.99), kind=kLoop, calls=%fused_computation.3 | loop fusion | flops 4423680 | bytes 5900288 | tf_op jit(solution)/shard_map/convert_element_type | solution.py:405
  80.5 1.6 copy-done.4
  82.1 0.0 copy-done.13
  82.1 1.0 convolution_convert_fusion.2
  83.1 0.0 copy-done.17
  83.1 0.0 slice-start
  83.2 0.0 slice-start.1
  83.2 5.7 %fusion.8 = f32[512,720]{0,1:T(8,128)S(1)} fusion(bf16[1,720,2880]{2,1,0:T(8,128)(2,1)} %param.18, bf16[512,2880]{1,0:T(8,128)(2,1)} %copy-done.4, f32[2880]{0:T(1024)S(1)} %reduce), kind=kOutput, calls=%fused_computation.9 | convolution fusion | flops 2127790080 | bytes 8582400 | tf_op jit(solution)/shard_map/dot_general | solution.py:15
  88.9 0.0 copy-done.9
  88.9 0.0 copy-start.8
  88.9 0.0 slice-start.2
  88.9 4.8 %multiply_add_fusion = f32[512,720]{0,1:T(8,128)S(1)} fusion(f32[512,720]{0,1:T(8,128)S(1)} %copy-done.9, bf16[512,2880]{1,0:T(8,128)(2,1)S(1)} %get-tuple-element.13, bf16[1,2,720,2880]{3,2,1,0:T(8,128)(2,1)} %param.16, f32[720]{0:T(1024)S(1)} %get-tuple-element.33), kind=kOutput, calls=%fused_computation.29 | convolution fusion | flops 2124472320 | bytes 10140480 | tf_op jit(solution)/shard_map/dot_general | solution.py:15
  93.8 0.0 copy-start.15
  93.8 2.5 %add_add_fusion = f32[512,720]{0,1:T(8,128)S(1)} fusion(f32[512,720]{0,1:T(8,128)S(1)} %copy-done.8, bf16[512,2880]{1,0:T(8,128)(2,1)S(1)} %get-tuple-element.13, bf16[1,2,720,2880]{3,2,1,0:T(8,128)(2,1)S(1)} %bitcast.103, f32[720]{0:T(1024)S(1)} %get-tuple-element.32), kind=kOutput, calls=%fused_computation.30 | convolution fusion | flops 2124840960 | bytes 10207232 | tf_op jit(solution)/shard_map/dot_general | solution.py:15
  96.3 1.2 multiply_convert_fusion.5
  97.5 0.0 copy-start.10
  97.6 0.0 copy-start.11
  97.6 0.0 copy-start.6
  97.6 0.2 fusion.15
  97.8 0.9 copy-done.10
  98.7 0.4 copy-done.11
  99.1 1.1 copy-done.5
  100.2 1.0 fusion.26
  101.2 0.9 convolution_convert_fusion
  102.1 0.0 all-reduce.4.cloned.1.call-update
  102.1 0.2 reduce-scatter.2.cloned.1.call-start
  102.3 10.9 %bitcast_convert_fusion = bf16[512,2880]{0,1:T(8,128)(2,1)} fusion(bf16[1,2,720,2880]{3,2,1,0:T(8,128)(2,1)} %param.16, f32[512,1,720]{0,2,1:T(8,128)} %copy-done.11, f32[512,1,720]{0,2,1:T(8,128)} %copy-done.10, f32[2,720]{1,0:T(2,128)S(1)} %bitcast.101), kind=kOutput, calls=%fused_computation.4 | convolution fusion | flops 4250419200 | bytes 14198400 | tf_op jit(solution)/shard_map/rjf,jfd->rd/dot_general | solution.py:453
  113.2 0.0 reduce-scatter.2.cloned.1.call-update
  113.3 1.5 fusion.28
  114.8 1.4 fusion.27
  116.2 0.0 copy-done.7
  116.2 0.3 fusion.45
  116.6 2.8 %all-reduce.4.cloned.1.call-done = (bf16[512,32]{0,1:T(8,128)(2,1)}, bf16[512,32]{0,1:T(8,128)(2,1)}) async-done(((bf16[512,32]{0,1:T(8,128)(2,1)}, bf16[512,32]{0,1:T(8,128)(2,1)}), (bf16[512,32]{0,1:T(8,128)(2,1)}, bf16[512,32]{0,1:T(8,128)(2,1)})) %all-reduce.4.cloned.1.call-update) | async-done | bytes 65552 | tf_op jit(solution)/shard_map/psum | solution.py:450
  119.4 1.4 fusion.18
  120.8 0.0 copy-done.16
  120.9 2.1 %fusion.16 = f32[32,1440]{1,0:T(8,128)S(1)} fusion(bf16[512,32]{0,1:T(8,128)(2,1)S(1)} %copy-done.16, bf16[512,2880]{1,0:T(8,128)(2,1)} %copy-done.4, s32[]{:T(128)S(6)} %select_n.14), kind=kOutput, calls=%fused_computation.20 | convolution fusion | flops 47185920 | bytes 1789956 | tf_op jit(solution)/shard_map/dot_general | solution.py:15
  123.0 10.5 %reduce-scatter.2.cloned.1.call-done = bf16[512,1440]{0,1:T(8,128)(2,1)} async-done(((bf16[512,2880]{0,1:T(8,128)(2,1)}), bf16[512,1440]{0,1:T(8,128)(2,1)}) %reduce-scatter.2.cloned.1.call-update) | async-done | bytes 1474576 | tf_op jit(solution)/shard_map/reduce_scatter | solution.py:456
  133.5 0.0 copy-done.14
  133.5 3.3 %fusion.14 = bf16[512,1440]{0,1:T(8,128)(2,1)} fusion(bf16[512,32]{0,1:T(8,128)(2,1)S(1)} %copy-done.14, bf16[512,1440]{0,1:T(8,128)(2,1)} %reduce-scatter.2.cloned.1.call-done, bf16[1,2880,32]{1,2,0:T(8,128)(2,1)S(1)} %copy-done, s32[]{:T(128)S(6)} %select_n.14), kind=kOutput, calls=%fused_computation.16 | convolution fusion | flops 50135040 | bytes 3080196 | tf_op jit(solution)/shard_map/dot_general | solution.py:15
  136.8 1.7 copy.36
  138.5 32.9 %shard_map.156 = (bf16[128,1440]{1,0:T(8,128)(2,1)S(1)}, f32[64,1440]{1,0:T(8,128)S(1)}, f32[96,720]{1,0:T(8,128)S(1)}) custom-call(bf16[4,128,1440]{2,1,0:T(8,128)(2,1)S(1)} %bitcast.96, bf16[64,1440]{1,0:T(8,128)(2,1)S(1)} %fusion.29.wide_ref, bf16[96,720]{1,0:T(8,128)(2,1)S(1)} %fusion.30.thin_ref), custom_call_target="tpu_custom_call" | custom-call | tf_op jit(solution)/shard_map/pallas_call | solution.py:293
  171.4 0.7 slice_bitcast_fusion.6
  172.1 0.8 copy.38
  172.9 0.8 slice_bitcast_fusion.4
  173.7 0.9 copy.37
  (28 shorter events, 0.2 us)
Async XLA Ops:
  7.2 65.9 %copy-start = (bf16[1,2880,32]{1,2,0:T(8,128)(2,1)S(1)}, bf16[1,2880,32]{1,2,0:T(8,128)(2,1)}, u32[]{:S(2)}) copy-start(bf16[1,2880,32]{1,2,0:T(8,128)(2,1)} %param.20) | copy-start | bytes 552964
  7.2 3.9 %copy-start.12 = (bf16[1,32,2,720]{3,2,1,0:T(2,128)(2,1)S(1)}, bf16[1,32,2,720]{3,2,1,0:T(2,128)(2,1)}, u32[]{:S(2)}) copy-start(bf16[1,32,2,720]{3,2,1,0:T(2,128)(2,1)} %param.21) | copy-start | bytes 276484
  7.2 3.9 %copy-start.19 = (f32[128,4]{0,1:T(4,128)S(1)}, f32[128,4]{0,1:T(4,128)}, u32[]{:S(2)}) copy-start(f32[128,4]{0,1:T(4,128)} %param.14) | copy-start | bytes 6148
  7.2 3.9 %copy-start.20 = (s32[128,4]{0,1:T(4,128)S(1)}, s32[128,4]{0,1:T(4,128)}, u32[]{:S(2)}) copy-start(s32[128,4]{0,1:T(4,128)} %param.15) | copy-start | bytes 6148
  7.2 112.2 %all-reduce.4.cloned.1.call-start = ((), (), s32[]{:S(2)}) async-start(), calls=%async_computation.2 | async-start | bytes 131072 | tf_op jit(solution)/shard_map/psum | solution.py:450
  11.2 1.0 copy-start.2
  12.2 1.0 copy-start.3
  73.1 1.6 copy-start.1
  74.7 3.1 %copy-start.18 = (f32[1,2,720]{2,1,0:T(2,128)S(1)}, f32[1,2,720]{2,1,0:T(2,128)}, u32[]{:S(2)}) copy-start(f32[1,2,720]{2,1,0:T(2,128)} %param.17) | copy-start | bytes 17284
  77.8 4.3 %copy-start.13 = (bf16[1,32,2880]{2,1,0:T(8,128)(2,1)S(1)}, bf16[1,32,2880]{2,1,0:T(8,128)(2,1)}, u32[]{:S(2)}) copy-start(bf16[1,32,2880]{2,1,0:T(8,128)(2,1)} %param.23) | copy-start | bytes 552964
  80.5 1.6 copy-start.4
  82.1 1.0 copy-start.17
  83.1 5.8 %copy-start.9 = (f32[512,720]{0,1:T(8,128)S(1)}, f32[512,720]{0,1:T(8,128)}, u32[]{:S(2)}) copy-start(f32[512,720]{0,1:T(8,128)} %fusion.35) | copy-start | bytes 4423684
  83.1 10.6 %slice-start = ((s8[8478720]{0:T(1024)(128)(4,1)}), s8[4194304]{0:T(1024)(128)(4,1)S(1)}, s32[]{:S(2)}) async-start(s8[8478720]{0:T(1024)(128)(4,1)} %bitcast.102), calls=%async_computation.3 | async-start | bytes 8388608
  83.2 10.6 %slice-start.1 = ((s8[8478720]{0:T(1024)(128)(4,1)}), s8[4194304]{0:T(1024)(128)(4,1)S(1)}, s32[]{:S(2)}) async-start(s8[8478720]{0:T(1024)(128)(4,1)} %bitcast.102), calls=%async_computation.4 | async-start | bytes 8388608
  88.9 4.8 %copy-start.8 = (f32[512,720]{0,1:T(8,128)S(1)}, f32[512,720]{0,1:T(8,128)}, u32[]{:S(2)}) copy-start(f32[512,720]{0,1:T(8,128)} %fusion.36) | copy-start | bytes 4423684
  88.9 4.8 %slice-start.2 = ((s8[8478720]{0:T(1024)(128)(4,1)}), s8[90112]{0:T(1024)(128)(4,1)S(1)}, s32[]{:S(2)}) async-start(s8[8478720]{0:T(1024)(128)(4,1)} %bitcast.102), calls=%async_computation.5 | async-start | bytes 180224
  93.8 2.5 %copy-start.15 = (bf16[1,720,32]{1,2,0:T(8,128)(2,1)S(1)}, bf16[1,720,32]{1,2,0:T(8,128)(2,1)}, u32[]{:S(2)}) copy-start(bf16[1,720,32]{1,2,0:T(8,128)(2,1)} %param.22) | copy-start | bytes 138244
  97.5 1.2 copy-start.10
  97.6 1.6 copy-start.11
  97.6 3.6 %copy-start.6 = (bf16[512,720]{0,1:T(8,128)(2,1)}, bf16[512,720]{0,1:T(8,128)(2,1)S(1)}, u32[]{:S(2)}) copy-start(bf16[512,720]{0,1:T(8,128)(2,1)S(1)} %get-tuple-element.36) | copy-start | bytes 2211844
  99.1 1.1 copy-start.5
  102.1 31.4 %reduce-scatter.2.cloned.1.call-start = ((), (), s32[]{:S(2)}) async-start(), calls=%async_computation.1 | async-start | bytes 4423680 | tf_op jit(solution)/shard_map/reduce_scatter | solution.py:456
  113.3 3.0 %copy-start.7 = (bf16[512,720]{0,1:T(8,128)(2,1)S(1)}, bf16[512,720]{0,1:T(8,128)(2,1)}, u32[]{:S(2)}) copy-start(bf16[512,720]{0,1:T(8,128)(2,1)} %copy-done.6) | copy-start | bytes 2211844
  119.4 1.4 copy-start.16
  120.8 12.6 %copy-start.14 = (bf16[512,32]{0,1:T(8,128)(2,1)S(1)}, bf16[512,32]{0,1:T(8,128)(2,1)}, u32[]{:S(2)}) copy-start(bf16[512,32]{0,1:T(8,128)(2,1)} %get-tuple-element.34) | copy-start | bytes 98308
Sparse Core Ops, SparseCore 0:
  102.2 17.1 all-reduce.3
  121.7 11.7 reduce-scatter.1

commit v3 on v2

--- a/solution.py
+++ b/solution.py
@@ -27,12 +27,13 @@
 
 
 def gather_kernel(
-    n, x_ref, dy_ref, w_ref, x_out, dy_out, w_out, held,
+    n, x_ref, dy_ref, w_ref, x_out, dy_out, w_out,
     line_send, line_recv, pair_send, pair_recv, w_send, w_recv,
 ):
     e = lax.axis_index("expert")
     c = lax.axis_index("tensor")
-    rows, width = x_ref.shape
+    width, rows = x_ref.shape
+    outs = (x_out, dy_out)
     barrier = pltpu.get_barrier_semaphore()
     for j in range(1, n):
         pl.semaphore_signal(
@@ -41,8 +42,14 @@
     pl.semaphore_signal(barrier, inc=1, device_id={"tensor": 1 - c}, device_id_type=MESH)
     pl.semaphore_wait(barrier, n)
 
+    def part(a, s, core):
+        return outs[a].at[
+            pl.ds(pl.multiple_of(core * width, width), width),
+            pl.ds(pl.multiple_of(s * rows, rows), rows),
+        ]
+
     def piece(a, s):
-        return held.at[a, s, c]
+        return part(a, s, c)
 
     def block(direction, k):
         return e - k if direction == 0 else e + k
@@ -74,7 +81,7 @@
         )
 
     def pair_in(a, s, slot):
-        other = held.at[a, s, 1 - c]
+        other = part(a, s, 1 - c)
         return remote(other, other, pair_send.at[a, slot], pair_recv.at[a, slot], tensor=1 - c)
 
     def own(a):
@@ -95,24 +102,17 @@
                         line(a, direction, k).start()
                 pair(a, block(direction, k), direction * (n - 1) + k).start()
 
-    def settle(a, out):
-        def lay(s):
-            where = pl.ds(pl.multiple_of(s * rows, rows), rows)
-            out[where, :] = jnp.concatenate([held[a, s, 0], held[a, s, 1]], axis=1)
-
+    def settle(a):
         pair_in(a, e, 0).wait_recv()
-        lay(e)
         for k in range(1, n):
             for direction in range(2):
                 @pl.when(arrives(direction, k))
                 def _():
-                    s = block(direction, k)
-                    pair_in(a, s, direction * (n - 1) + k).wait_recv()
-                    lay(s)
-
-    held[0, e, c] = x_ref[...]
+                    pair_in(a, block(direction, k), direction * (n - 1) + k).wait_recv()
+
+    piece(0, e)[...] = x_ref[...]
     own(0)
-    held[1, e, c] = dy_ref[...]
+    piece(1, e)[...] = dy_ref[...]
     for j in range(1, n):
         remote(
             w_ref, w_out.at[e], w_send.at[j], w_recv.at[j], expert=lax.rem(e + j, n)
@@ -123,10 +123,10 @@
     for k in range(2, n):
         hop(0, k)
     hop(1, 1)
-    settle(0, x_out)
     for k in range(2, n):
         hop(1, k)
-    settle(1, dy_out)
+    settle(0)
+    settle(1)
     for j in range(1, n):
         source = lax.rem(e + n - j, n)
         remote(
@@ -151,15 +151,14 @@
 def gather_rows(x, dy, w):
     n = lax.axis_size("expert")
     cores = lax.axis_size("tensor")
-    rows, width = x.shape
-    whole = jax.ShapeDtypeStruct((n * rows, cores * width), x.dtype)
+    width, rows = x.shape
+    whole = jax.ShapeDtypeStruct((cores * width, n * rows), x.dtype)
     return pl.pallas_call(
         functools.partial(gather_kernel, n),
         out_shape=(whole, whole, jax.ShapeDtypeStruct((n,) + w.shape, w.dtype)),
         in_specs=[pl.BlockSpec(memory_space=pltpu.VMEM)] * 3,
         out_specs=[pl.BlockSpec(memory_space=pltpu.VMEM)] * 3,
         scratch_shapes=[
-            pltpu.VMEM((2, n, cores, rows, width), x.dtype),
             pltpu.SemaphoreType.DMA((2, 2, n)),
             pltpu.SemaphoreType.DMA((2, 2, n)),
             pltpu.SemaphoreType.DMA((2, 2 * n)),
@@ -174,11 +173,12 @@
 
 
 def return_kernel(
-    n, m, rows_ref, wide_ref, thin_ref, out_ref, wide_out, thin_out,
-    from_up, from_down, summed, wide_in, thin_in,
-    line_send, line_recv, peer_send, peer_recv,
+    n, m, part_ref, wide_ref, thin_ref, out_ref, wide_out, thin_out,
+    from_up, from_down, summed, wide_in, thin_in, rows_ref, other_in,
+    line_send, line_recv, peer_send, peer_recv, pair_send, pair_recv,
 ):
     e = lax.axis_index("expert")
+    c = lax.axis_index("tensor")
     d = lax.axis_index("dp")
     wide_type = jnp.float32
     barrier = pltpu.get_barrier_semaphore()
@@ -190,7 +190,30 @@
         pl.semaphore_signal(
             barrier, inc=1, device_id={"dp": lax.rem(d + j, m)}, device_id_type=MESH
         )
-    pl.semaphore_wait(barrier, n + m - 2)
+    pl.semaphore_signal(barrier, inc=1, device_id={"tensor": 1 - c}, device_id_type=MESH)
+    half, rows = out_ref.shape
+
+    order = tuple(t for i in range((n + 1) // 2) for t in dict.fromkeys((i, n - 1 - i)))
+
+    def part(t, core):
+        return part_ref.at[
+            pl.ds(pl.multiple_of(core * half, half), half), pl.ds(t * rows, rows)
+        ]
+
+    def exchange(t):
+        return remote(
+            part(t, 1 - c), other_in.at[t], pair_send.at[t], pair_recv.at[t], tensor=1 - c
+        )
+
+    pl.semaphore_wait(barrier, n + m - 1)
+    for t in order:
+        exchange(t).start()
+
+    def join(t):
+        exchange(t).wait_recv()
+        rows_ref[t] = (part(t, c)[...].astype(wide_type) + other_in[t].astype(wide_type)).astype(
+            rows_ref.dtype
+        )
 
     landing = (from_up, from_down)
 
@@ -236,7 +259,11 @@
                 ).astype(summed.dtype)
                 outgoing(direction, t, summed.at[t]).start()
 
+    for t in order[:2]:
+        join(t)
     line_step(0)
+    for t in order[2:]:
+        join(t)
     pieces = ((wide_ref, wide_in), (thin_ref, thin_in))
     for j in range(1, m):
         for i, (src, dst) in enumerate(pieces):
@@ -278,6 +305,8 @@
             + from_down[e].astype(wide_type)
         ).astype(out_ref.dtype)
 
+    for t in order:
+        exchange(t).wait_send()
     for step in range(n - 1):
         for direction in range(2):
             @pl.when(sends(direction, step))
@@ -289,7 +318,8 @@
 def return_rows(dx, wide, thin):
     n = lax.axis_size("expert")
     m = lax.axis_size("dp")
-    shape = (n, dx.shape[0] // n, dx.shape[1])
+    cores = lax.axis_size("tensor")
+    shape = (n, dx.shape[0] // cores, dx.shape[1] // n)
     return pl.pallas_call(
         functools.partial(return_kernel, n, m),
         out_shape=(
@@ -305,15 +335,19 @@
             pltpu.VMEM(shape, dx.dtype),
             pltpu.VMEM((m - 1,) + wide.shape, wide.dtype),
             pltpu.VMEM((m - 1,) + thin.shape, thin.dtype),
+            pltpu.VMEM(shape, dx.dtype),
+            pltpu.VMEM(shape, dx.dtype),
             pltpu.SemaphoreType.DMA((n,)),
             pltpu.SemaphoreType.DMA((2, n)),
             pltpu.SemaphoreType.DMA((2, m)),
             pltpu.SemaphoreType.DMA((2, m)),
+            pltpu.SemaphoreType.DMA((n,)),
+            pltpu.SemaphoreType.DMA((n,)),
         ],
         compiler_params=pltpu.CompilerParams(
             collective_id=1, has_side_effects=True, vmem_limit_bytes=32 * 2**20
         ),
-    )(dx.reshape(shape), wide, thin)
+    )(dx, wide, thin)
 
 
 def shards(
@@ -345,6 +379,8 @@
         and capacity == tok_rows
         and local_count == 1
         and lax.axis_size("tensor") == 2
+        and tok_rows % 128 == 0
+        and gradient_slice % 16 == 0
     )
     if dense:
         expert_ids = jnp.arange(experts_all, dtype=jnp.int32)
@@ -358,10 +394,12 @@
         )
         spread = jnp.zeros((-(-experts_all // 8) * 8, tok_rows), jnp.float32)
         spread = lax.dynamic_update_slice(spread, token_weight.T, (0, 0))
-        rows_x, rows_dy, weights = gather_rows(activations, output_gradient, spread)
+        rows_x, rows_dy, weights = gather_rows(
+            activations.T, output_gradient.T, spread
+        )
         mine = lax.axis_index("expert")
         recv_w = lax.dynamic_slice_in_dim(weights, mine, 1, 1).reshape(1, -1)
-        recv_x, recv_dy = rows_x[None], rows_dy[None]
+        recv_x, recv_dy = rows_x.T[None], rows_dy.T[None]
     else:
         flat_experts = token_experts.reshape(tok_rows * top_count)
         onehot = (flat_experts[:, None] == jnp.arange(experts_all, dtype=jnp.int32)[None, :]).astype(
@@ -453,16 +491,23 @@
     partial_value = jnp.einsum(
         "rjf,jfd->rd", dz_scaled, gate_up_weight[0], preferred_element_type=single_float
     )
-    summed_values = lax.psum_scatter(
-        partial_value.astype(jnp.bfloat16), "tensor", scatter_dimension=1, tiled=True
-    ).astype(jnp.float32)
-    input_first_rows = lax.dynamic_slice_in_dim(
-        adapter_input_first[0], gradient_start, gradient_slice, 0
-    )
-    input_gradient_rows = (
-        summed_values + ADAPTER_SCALE * contract_product(input_adapter, input_first_rows, 1, 1)
-    ).astype(brain_float_half)
-    dx_list = [input_gradient_rows]
+    if dense:
+        partial_rows = (
+            partial_value
+            + ADAPTER_SCALE
+            * contract_product(input_portion.astype(brain_float_half), adapter_input_first[0], 1, 1)
+        ).astype(brain_float_half)
+    else:
+        summed_values = lax.psum_scatter(
+            partial_value.astype(jnp.bfloat16), "tensor", scatter_dimension=1, tiled=True
+        ).astype(jnp.float32)
+        input_first_rows = lax.dynamic_slice_in_dim(
+            adapter_input_first[0], gradient_start, gradient_slice, 0
+        )
+        input_gradient_rows = (
+            summed_values + ADAPTER_SCALE * contract_product(input_adapter, input_first_rows, 1, 1)
+        ).astype(brain_float_half)
+        dx_list = [input_gradient_rows]
     input_columns = lax.dynamic_slice_in_dim(input_rows, gradient_start, gradient_slice, 1)
     gradient_columns = lax.dynamic_slice_in_dim(gradient_rows, gradient_start, gradient_slice, 1)
     if dense:
@@ -484,12 +529,12 @@
             axis=0,
         )
         input_grad, wide_sum, thin_sum = return_rows(
-            dx_list[0],
+            partial_rows.T,
             (ADAPTER_SCALE * wide).astype(brain_float_half),
             (ADAPTER_SCALE * thin).astype(brain_float_half),
         )
         return (
-            input_grad,
+            input_grad.T,
             wide_sum[:rank].T[None],
             jnp.stack([thin_sum[:rank], thin_sum[rank : 2 * rank]], axis=1)[None],
             thin_sum[2 * rank :].T[None],

time: 182 us -> 171 us (0.940)
  matrix products: 42 us -> 34 us
  local copies, waits for them, and re-layouts: 15.5 us -> 9.81 us
  waiting for transfers between devices: 13.3 us -> 15.6 us
    psum x1, waiting for transfers between devices: 2.83 us -> 15.1 us  [shards(): lax.psum(down_portion.astype(jnp.bfloat16), 'tensor').astype(jnp.float32)]
    reduce_scatter x1 -> x0, waiting for transfers between devices: 10.5 us -> none  [shards(): lax.psum_scatter(partial_value.astype(jnp.bfloat16), 'tensor', scatter_di...]
    dot_general x11, matrix products: 25.3 us -> 21 us  [contract_product(): lax.dot_general(left, right, (((left_dim,), (right_dim,)), ((), ())), pre...]
    unnamed x53 -> x45, local copies, waits for them, and re-layouts: 12.4 us -> 8.34 us
    pallas_call x1, Pallas kernels: 59.9 us -> 56.7 us  [gather_rows(): pl.pallas_call(functools.partial(gather_kernel, n), out_shape=(whole, who...]
    dot_general x1, matrix products: 10.9 us -> 8.05 us  [shards(): jnp.einsum('rjf,jfd->rd', dz_scaled, gate_up_weight[0], preferred_element...]
    pallas_call x1, Pallas kernels: 32.9 us -> 35.4 us  [return_rows(): pl.pallas_call(functools.partial(return_kernel, n, m), out_shape=(jax.Sha...]
  transfers between devices with their start and end apart: 2 -> 1, of which waited for: 2 -> 1; matrix products, arithmetic and copies ran while one was open for 10% -> 3% of each run, Pallas kernels for 0% -> 0%
where the time goes in v3:
time: 171 us
  Pallas kernels  92.1 us (54%)
  matrix products  34 us (20%)
  waiting for transfers between devices  15.6 us (9%)
  between operations  14.4 us (8%)
  local copies, waits for them, and re-layouts  9.81 us (6%)
  other arithmetic  4.42 us (3%)
    pallas_call x1, Pallas kernels, gather_rows(): pl.pallas_call(functools.partial(gather_kernel, n), out_shape=(whole, who...  56.7 us
    pallas_call x1, Pallas kernels, return_rows(): pl.pallas_call(functools.partial(return_kernel, n, m), out_shape=(jax.Sha...  35.4 us
    dot_general x11, matrix products, contract_product(): lax.dot_general(left, right, (((left_dim,), (right_dim,)), ((), ())), pre...  21 us
    psum x1, waiting for transfers between devices, shards(): lax.psum(down_portion.astype(jnp.bfloat16), 'tensor').astype(jnp.float32)  15.1 us
    unnamed x45, local copies, waits for them, and re-layouts  8.34 us
    dot_general x1, matrix products, shards(): jnp.einsum('rjf,jfd->rd', dz_scaled, gate_up_weight[0], preferred_element...  8.05 us
  transfers between devices with their start and end apart: 1, of which 1 were waited for; matrix products, arithmetic and copies ran while one was open for 3% of the time, Pallas kernels for 0%

profile of v3, /device:TPU:0, one launch (start us, length us, event | category | flops | bytes accessed | tf_op | source)
XLA Modules:
  0.0 170.5 jit_solution(14301134842810986748)
XLA Ops:
  7.2 0.0 copy-start
  7.2 0.9 copy.29
  8.1 0.7 select_reduce_fusion
  8.9 1.0 copy-done.3
  9.8 1.0 copy-done.4
  10.8 56.7 %shard_map.155 = (bf16[2880,512]{1,0:T(8,128)(2,1)S(1)}, bf16[2880,512]{1,0:T(8,128)(2,1)S(1)}, f32[4,8,128]{2,1,0:T(8,128)S(1)}) custom-call(bf16[1440,128]{1,0:T(8,128)(2,1)S(1)} %bitcast.101, bf16[1440,128]{1,0:T(8,128)(2,1)S(1)} %bitcast.102, f32[8,128]{1,0:T(8,128)S(1)} %dynamic_update_slice.3.w_ref), custom_call_target="tpu_custom_call" | custom-call | tf_op jit(solution)/shard_map/pallas_call | solution.py:156
  67.6 0.0 copy-start.2
  67.6 1.6 copy-done.2
  69.2 0.0 copy-done
  69.2 0.6 convolution_convert_fusion.1
  69.8 0.0 copy-start.16
  69.8 1.6 fusion.32
  71.4 1.5 fusion.33
  72.9 0.0 copy-done.17
  73.0 0.0 copy-done.16
  73.0 0.0 copy-start.13
  73.0 0.0 slice-start
  73.1 2.5 %multiply_convert_fusion.1 = bf16[2880,512]{1,0:T(8,128)(2,1)S(1)} fusion(bf16[2880,512]{1,0:T(8,128)(2,1)} %copy-done.2, f32[512]{0:T(512)S(1)} %bitcast.106), kind=kLoop, calls=%fused_computation.5 | loop fusion | flops 4423680 | bytes 5900288 | tf_op jit(solution)/shard_map/convert_element_type | solution.py:443
  75.5 0.0 copy-done.13
  75.5 0.0 copy-start.5
  75.6 0.0 slice-start.1
  75.6 0.6 convolution_convert_fusion.2
  76.2 1.0 copy-done.5
  77.2 5.5 %fusion.7 = f32[512,720]{0,1:T(8,128)S(1)} fusion(bf16[1,720,2880]{2,1,0:T(8,128)(2,1)} %param.18, bf16[2880,512]{1,0:T(8,128)(2,1)S(1)} %multiply_convert_fusion.1, f32[2880]{0:T(1024)S(1)} %reduce), kind=kOutput, calls=%fused_computation.10 | convolution fusion | flops 2127790080 | bytes 8582400 | tf_op jit(solution)/shard_map/dot_general | solution.py:15
  82.7 0.0 slice-done
  82.7 0.0 slice-done.1
  82.7 0.0 copy-done.10
  82.7 0.0 slice-done.2
  82.7 0.0 copy-start.9
  82.7 2.4 %multiply_add_fusion = f32[512,720]{0,1:T(8,128)S(1)} fusion(f32[512,720]{0,1:T(8,128)S(1)} %copy-done.10, bf16[2880,512]{1,0:T(8,128)(2,1)S(1)} %get-tuple-element.13, bf16[1,2,720,2880]{3,2,1,0:T(8,128)(2,1)S(1)} %bitcast.110, f32[720]{0:T(1024)S(1)} %get-tuple-element.33), kind=kOutput, calls=%fused_computation.28 | convolution fusion | flops 2124472320 | bytes 10141696 | tf_op jit(solution)/shard_map/dot_general | solution.py:15
  85.2 0.0 copy-done.1
  85.2 0.0 copy-done.9
  85.2 0.0 copy-start.14
  85.2 2.4 %add_add_fusion = f32[512,720]{0,1:T(8,128)S(1)} fusion(f32[512,720]{0,1:T(8,128)S(1)} %copy-done.9, bf16[2880,512]{1,0:T(8,128)(2,1)S(1)} %get-tuple-element.13, bf16[1,2,720,2880]{3,2,1,0:T(8,128)(2,1)S(1)} %bitcast.110, f32[720]{0:T(1024)S(1)} %get-tuple-element.32), kind=kOutput, calls=%fused_computation.29 | convolution fusion | flops 2124840960 | bytes 10141696 | tf_op jit(solution)/shard_map/dot_general | solution.py:15
  87.6 0.0 copy-done.14
  87.7 1.2 multiply_convert_fusion.5
  88.9 0.0 copy-start.8
  88.9 0.9 convolution_convert_fusion
  89.8 0.0 copy-done.8
  89.8 0.2 fusion.13
  90.1 0.0 copy-start.6
  90.1 1.1 copy-done.6
  91.2 0.0 copy-done.11
  91.2 0.3 fusion.24
  91.6 8.1 %fusion = f32[512,2880,1]{0,1,2:T(8,128)S(1)} fusion(bf16[1,2,720,2880]{3,2,1,0:T(8,128)(2,1)} %param.16, f32[512,1,720]{0,2,1:T(8,128)S(1)} %get-tuple-element.38, f32[512,1,720]{0,2,1:T(8,128)S(1)} %get-tuple-element.37, f32[2,720]{1,0:T(2,128)S(1)} %bitcast.108), kind=kOutput, calls=%fused_computation | convolution fusion | flops 4248944640 | bytes 17147520 | tf_op jit(solution)/shard_map/rjf,jfd->rd/dot_general | solution.py:491
  99.6 0.0 copy-done.12
  99.6 1.0 fusion.11.part_ref
  100.6 0.2 all-reduce.4.cloned.1.call-start
  100.8 0.5 all-reduce.4.cloned.1.call-update
  101.3 0.0 copy-start.7
  101.3 1.5 fusion.41
  102.9 1.4 fusion.25
  104.3 0.0 copy-done.7
  104.4 1.0 fusion.26
  105.3 0.9 fusion.28.thin_ref
  106.2 15.1 %all-reduce.4.cloned.1.call-done = (bf16[512,32]{0,1:T(8,128)(2,1)}, bf16[512,32]{0,1:T(8,128)(2,1)}) async-done(((bf16[512,32]{0,1:T(8,128)(2,1)}, bf16[512,32]{0,1:T(8,128)(2,1)}), (bf16[512,32]{0,1:T(8,128)(2,1)}, bf16[512,32]{0,1:T(8,128)(2,1)})) %all-reduce.4.cloned.1.call-update) | async-done | bytes 65552 | tf_op jit(solution)/shard_map/psum | solution.py:468
  121.3 1.9 %fusion.16 = f32[32,1440]{1,0:T(8,128)S(1)} fusion(bf16[512,32]{0,1:T(8,128)(2,1)} %get-tuple-element.35, bf16[2880,512]{1,0:T(8,128)(2,1)} %copy-done.1, s32[]{:T(128)S(6)} %select_n.13), kind=kOutput, calls=%fused_computation.22 | convolution fusion | flops 47185920 | bytes 1691652 | tf_op jit(solution)/shard_map/dot_general | solution.py:15
  123.3 0.0 copy-done.15
  123.3 1.9 %fusion.14 = f32[32,1440]{1,0:T(8,128)S(1)} fusion(bf16[512,32]{0,1:T(8,128)(2,1)S(1)} %copy-done.15, bf16[2880,512]{1,0:T(8,128)(2,1)} %copy-done.5, s32[]{:T(128)S(6)} %select_n.13), kind=kOutput, calls=%fused_computation.19 | convolution fusion | flops 47185920 | bytes 1691652 | tf_op jit(solution)/shard_map/dot_general | solution.py:15
  125.3 35.4 %shard_map.156 = (bf16[1440,128]{1,0:T(8,128)(2,1)S(1)}, f32[64,1440]{1,0:T(8,128)S(1)}, f32[96,720]{1,0:T(8,128)S(1)}) custom-call(bf16[2880,512]{1,0:T(8,128)(2,1)S(1)} %fusion.11.part_ref, bf16[64,1440]{1,0:T(8,128)(2,1)S(1)} %fusion.27.wide_ref, bf16[96,720]{1,0:T(8,128)(2,1)S(1)} %fusion.28.thin_ref), custom_call_target="tpu_custom_call" | custom-call | tf_op jit(solution)/shard_map/pallas_call | solution.py:323
  160.7 0.7 slice_bitcast_fusion.6
  161.3 0.8 copy.26
  162.2 0.8 slice_bitcast_fusion.4
  162.9 0.7 copy.33
  (16 shorter events, 0.1 us)
Async XLA Ops:
  7.2 62.0 %copy-start = (bf16[1,2880,32]{1,2,0:T(8,128)(2,1)S(1)}, bf16[1,2880,32]{1,2,0:T(8,128)(2,1)}, u32[]{:S(2)}) copy-start(bf16[1,2880,32]{1,2,0:T(8,128)(2,1)} %param.20) | copy-start | bytes 552964
  8.9 1.0 copy-start.3
  9.8 1.0 copy-start.4
  67.6 1.6 copy-start.2
  69.2 16.0 %copy-start.1 = (bf16[2880,512]{1,0:T(8,128)(2,1)}, bf16[2880,512]{1,0:T(8,128)(2,1)S(1)}, u32[]{:S(2)}) copy-start(bf16[2880,512]{1,0:T(8,128)(2,1)S(1)} %get-tuple-element.13) | copy-start | bytes 8847364
  69.8 3.2 %copy-start.17 = (f32[1,2,720]{2,1,0:T(2,128)S(1)}, f32[1,2,720]{2,1,0:T(2,128)}, u32[]{:S(2)}) copy-start(f32[1,2,720]{2,1,0:T(2,128)} %param.17) | copy-start | bytes 17284
  69.8 3.2 %copy-start.16 = (f32[1,2880]{1,0:T(1,128)S(1)}, f32[1,2880]{1,0:T(1,128)}, u32[]{:S(2)}) copy-start(f32[1,2880]{1,0:T(1,128)} %param.19) | copy-start | bytes 34564
  73.0 2.5 %copy-start.13 = (bf16[1,32,2880]{2,1,0:T(8,128)(2,1)S(1)}, bf16[1,32,2880]{2,1,0:T(8,128)(2,1)}, u32[]{:S(2)}) copy-start(bf16[1,32,2880]{2,1,0:T(8,128)(2,1)} %param.23) | copy-start | bytes 552964
  73.0 9.6 %slice-start = ((s8[8478720]{0:T(1024)(128)(4,1)}), s8[90112]{0:T(1024)(128)(4,1)S(1)}, s32[]{:S(2)}) async-start(s8[8478720]{0:T(1024)(128)(4,1)} %bitcast.109), calls=%async_computation.1 | async-start | bytes 180224
  75.5 1.6 copy-start.5
  75.6 7.1 %slice-start.1 = ((s8[8478720]{0:T(1024)(128)(4,1)}), s8[4194304]{0:T(1024)(128)(4,1)S(1)}, s32[]{:S(2)}) async-start(s8[8478720]{0:T(1024)(128)(4,1)} %bitcast.109), calls=%async_computation.2 | async-start | bytes 8388608
  77.2 5.5 %copy-start.10 = (f32[512,720]{0,1:T(8,128)S(1)}, f32[512,720]{0,1:T(8,128)}, u32[]{:S(2)}) copy-start(f32[512,720]{0,1:T(8,128)} %fusion.32) | copy-start | bytes 4423684
  77.2 5.5 %slice-start.2 = ((s8[8478720]{0:T(1024)(128)(4,1)}), s8[4194304]{0:T(1024)(128)(4,1)S(1)}, s32[]{:S(2)}) async-start(s8[8478720]{0:T(1024)(128)(4,1)} %bitcast.109), calls=%async_computation.3 | async-start | bytes 8388608
  82.7 2.5 %copy-start.9 = (f32[512,720]{0,1:T(8,128)S(1)}, f32[512,720]{0,1:T(8,128)}, u32[]{:S(2)}) copy-start(f32[512,720]{0,1:T(8,128)} %fusion.33) | copy-start | bytes 4423684
  85.2 2.5 %copy-start.14 = (bf16[1,720,32]{1,2,0:T(8,128)(2,1)S(1)}, bf16[1,720,32]{1,2,0:T(8,128)(2,1)}, u32[]{:S(2)}) copy-start(bf16[1,720,32]{1,2,0:T(8,128)(2,1)} %param.22) | copy-start | bytes 138244
  88.9 0.9 copy-start.8
  89.8 1.4 copy-start.11
  90.1 1.1 copy-start.6
  91.6 8.1 %copy-start.12 = (bf16[512,32]{0,1:T(8,128)(2,1)}, bf16[512,32]{0,1:T(8,128)(2,1)S(1)}, u32[]{:S(2)}) copy-start(bf16[512,32]{0,1:T(8,128)(2,1)S(1)} %fusion.24) | copy-start | bytes 98308
  100.6 20.7 %all-reduce.4.cloned.1.call-start = ((), (), s32[]{:S(2)}) async-start(), calls=%async_computation | async-start | bytes 131072 | tf_op jit(solution)/shard_map/psum | solution.py:468
  101.3 3.0 %copy-start.7 = (bf16[512,2,720]{0,2,1:T(8,128)(2,1)S(1)}, bf16[512,2,720]{0,2,1:T(8,128)(2,1)}, u32[]{:S(2)}) copy-start(bf16[512,2,720]{0,2,1:T(8,128)(2,1)} %copy-done.6) | copy-start | bytes 4423684
  121.3 1.9 %copy-start.15 = (bf16[512,32]{0,1:T(8,128)(2,1)S(1)}, bf16[512,32]{0,1:T(8,128)(2,1)}, u32[]{:S(2)}) copy-start(bf16[512,32]{0,1:T(8,128)(2,1)} %get-tuple-element.34) | copy-start | bytes 98308
Sparse Core Ops, SparseCore 0:
  104.3 16.9 all-reduce.3

commit v4 on v3

--- a/solution.py
+++ b/solution.py
@@ -465,7 +465,6 @@
     glu = gate_values * sig
     hidden_units = ((up_activation + 1.0) * glu).astype(brain_float_half)
     down_portion = jnp.dot(hidden_units, adapter_down_first[0], preferred_element_type=single_float)
-    down_sum = lax.psum(down_portion.astype(jnp.bfloat16), "tensor").astype(jnp.float32)
     backward_adapter = contract_product(gradient_rows, adapter_down_second[0], 1, 1).astype(
         brain_float_half
     )
@@ -485,7 +484,14 @@
         adapter_input_second[0],
         preferred_element_type=single_float,
     )
-    in_sum = lax.psum(input_portion.astype(jnp.bfloat16), "tensor").astype(jnp.float32)
+    if dense:
+        own_low = jnp.concatenate([down_portion.T, input_portion.T], axis=0).astype(jnp.bfloat16)
+        pair_low = lax.ppermute(own_low, "tensor", [(0, 1), (1, 0)])
+        low_sum = (own_low.astype(jnp.float32) + pair_low.astype(jnp.float32)).T
+        down_sum, in_sum = jnp.split(low_sum, 2, axis=1)
+    else:
+        down_sum = lax.psum(down_portion.astype(jnp.bfloat16), "tensor").astype(jnp.float32)
+        in_sum = lax.psum(input_portion.astype(jnp.bfloat16), "tensor").astype(jnp.float32)
     down_adapter = down_sum.astype(brain_float_half)
     input_adapter = in_sum.astype(brain_float_half)
     partial_value = jnp.einsum(

time: 171 us -> 139 us (0.81)
  waiting for transfers between devices: 15.6 us -> 0.01 us
  between operations: 14.4 us -> 0.96 us
  matrix products: 34 us -> 30.9 us
    psum x1 -> x0, waiting for transfers between devices: 15.1 us -> none  [shards(): lax.psum(down_portion.astype(jnp.bfloat16), 'tensor').astype(jnp.float32)]
    dot_general x11, matrix products: 21 us -> 18.2 us  [contract_product(): lax.dot_general(left, right, (((left_dim,), (right_dim,)), ((), ())), pre...]
    unnamed x45 -> x41, local copies, waits for them, and re-layouts: 8.34 us -> 8.67 us
  transfers between devices with their start and end apart: 1 -> 1, of which waited for: 1 -> 0; matrix products, arithmetic and copies ran while one was open for 3% -> 7% of each run, Pallas kernels for 0% -> 0%
where the time goes in v4:
time: 139 us; the launch traced here: 138 us
  Pallas kernels  90.7 us (65%)
  matrix products  30.9 us (22%)
  local copies, waits for them, and re-layouts  10.1 us (7%)
  other arithmetic  5.07 us (4%)
    pallas_call x1, Pallas kernels, gather_rows(): pl.pallas_call(functools.partial(gather_kernel, n), out_shape=(whole, who...  56.7 us
    pallas_call x1, Pallas kernels, return_rows(): pl.pallas_call(functools.partial(return_kernel, n, m), out_shape=(jax.Sha...  34 us
    dot_general x11, matrix products, contract_product(): lax.dot_general(left, right, (((left_dim,), (right_dim,)), ((), ())), pre...  18.2 us
    unnamed x41, local copies, waits for them, and re-layouts  8.67 us
    dot_general x1, matrix products, shards(): jnp.einsum('rjf,jfd->rd', dz_scaled, gate_up_weight[0], preferred_element...  8.42 us
  transfers between devices with their start and end apart: 1, of which 0 were waited for; matrix products, arithmetic and copies ran while one was open for 7% of the time, Pallas kernels for 0%

profile of v4, /device:TPU:0, one launch (start us, length us, event | category | flops | bytes accessed | tf_op | source)
XLA Modules:
  0.0 138.1 jit_solution(14836066458230581948)
XLA Ops:
  0.6 0.0 copy-start
  0.6 0.9 copy.29
  1.6 0.7 select_reduce_fusion
  2.3 0.0 copy-start.3
  2.3 1.0 copy-done.3
  3.3 0.0 copy-start.4
  3.3 1.0 copy-done.4
  4.3 56.7 %shard_map.155 = (bf16[2880,512]{1,0:T(8,128)(2,1)S(1)}, bf16[2880,512]{1,0:T(8,128)(2,1)S(1)}, f32[4,8,128]{2,1,0:T(8,128)S(1)}) custom-call(bf16[1440,128]{1,0:T(8,128)(2,1)S(1)} %bitcast.104, bf16[1440,128]{1,0:T(8,128)(2,1)S(1)} %bitcast.105, f32[8,128]{1,0:T(8,128)S(1)} %dynamic_update_slice.3.w_ref), custom_call_target="tpu_custom_call" | custom-call | tf_op jit(solution)/shard_map/pallas_call | solution.py:156
  61.0 0.0 copy-start.2
  61.0 1.6 %copy-done.2 = bf16[2880,512]{1,0:T(8,128)(2,1)} copy-done((bf16[2880,512]{1,0:T(8,128)(2,1)}, bf16[2880,512]{1,0:T(8,128)(2,1)S(1)}, u32[]{:S(2)}) %copy-start.2) | copy-done | bytes 2949144
  62.6 0.0 copy-done
  62.6 0.6 convolution_convert_fusion.1
  63.2 0.0 copy-start.14
  63.2 1.6 %fusion.34 = f32[512,720]{0,1:T(8,128)} fusion(bf16[512,32]{0,1:T(8,128)(2,1)S(1)} %convolution_convert_fusion.1, bf16[32,2,720]{2,0,1:T(8,128)(2,1)S(1)} %bitcast.109), kind=kOutput, calls=%fused_computation.60 | convolution fusion | flops 23592960 | bytes 1556480 | tf_op jit(solution)/shard_map/dot_general | solution.py:454
  64.9 1.5 %fusion.35 = f32[512,720]{0,1:T(8,128)} fusion(bf16[512,32]{0,1:T(8,128)(2,1)S(1)} %convolution_convert_fusion.1, bf16[32,2,720]{2,0,1:T(8,128)(2,1)S(1)} %bitcast.110), kind=kOutput, calls=%fused_computation.62 | convolution fusion | flops 23592960 | bytes 1556480 | tf_op jit(solution)/shard_map/dot_general | solution.py:461
  66.4 0.0 copy-done.15
  66.4 0.0 copy-done.14
  66.5 0.0 copy-start.12
  66.5 0.0 slice-start
  66.5 2.5 %multiply_convert_fusion.1 = bf16[2880,512]{1,0:T(8,128)(2,1)S(1)} fusion(bf16[2880,512]{1,0:T(8,128)(2,1)} %copy-done.2, f32[512]{0:T(512)S(1)} %bitcast.111), kind=kLoop, calls=%fused_computation.5 | loop fusion | flops 4423680 | bytes 5900288 | tf_op jit(solution)/shard_map/convert_element_type | solution.py:443
  69.0 0.0 copy-done.12
  69.0 0.0 copy-start.5
  69.0 0.0 slice-start.1
  69.0 0.6 convolution_convert_fusion.2
  69.6 1.0 copy-done.5
  70.6 5.5 %fusion.7 = f32[512,720]{0,1:T(8,128)S(1)} fusion(bf16[1,720,2880]{2,1,0:T(8,128)(2,1)} %param.18, bf16[2880,512]{1,0:T(8,128)(2,1)S(1)} %multiply_convert_fusion.1, f32[2880]{0:T(1024)S(1)} %reduce), kind=kOutput, calls=%fused_computation.10 | convolution fusion | flops 2127790080 | bytes 8582400 | tf_op jit(solution)/shard_map/dot_general | solution.py:15
  76.1 0.0 slice-done
  76.1 0.0 slice-done.1
  76.1 0.0 copy-done.10
  76.1 0.0 slice-done.2
  76.2 0.0 copy-start.6
  76.2 2.4 %multiply_add_fusion = f32[512,720]{0,1:T(8,128)S(1)} fusion(f32[512,720]{0,1:T(8,128)S(1)} %copy-done.10, bf16[2880,512]{1,0:T(8,128)(2,1)S(1)} %get-tuple-element.13, bf16[1,2,720,2880]{3,2,1,0:T(8,128)(2,1)S(1)} %bitcast.115, f32[720]{0:T(1024)S(1)} %get-tuple-element.33), kind=kOutput, calls=%fused_computation.28 | convolution fusion | flops 2124472320 | bytes 10141696 | tf_op jit(solution)/shard_map/dot_general | solution.py:15
  78.6 0.0 copy-done.1
  78.6 0.0 copy-done.6
  78.6 0.0 copy-start.13
  78.6 2.4 %add_add_fusion = f32[512,720]{0,1:T(8,128)S(1)} fusion(f32[512,720]{0,1:T(8,128)S(1)} %copy-done.6, bf16[2880,512]{1,0:T(8,128)(2,1)S(1)} %get-tuple-element.13, bf16[1,2,720,2880]{3,2,1,0:T(8,128)(2,1)S(1)} %bitcast.115, f32[720]{0:T(1024)S(1)} %get-tuple-element.32), kind=kOutput, calls=%fused_computation.29 | convolution fusion | flops 2124840960 | bytes 10141696 | tf_op jit(solution)/shard_map/dot_general | solution.py:15
  81.1 0.0 copy-done.13
  81.1 1.4 %multiply_convert_fusion.5 = (bf16[512,720]{0,1:T(8,128)(2,1)S(1)}, f32[512,1,720]{0,2,1:T(8,128)S(1)}, f32[512,1,720]{0,2,1:T(8,128)S(1)}) fusion(f32[512,720]{0,1:T(8,128)S(1)} %add_add_fusion, f32[512,720]{0,1:T(8,128)S(1)} %multiply_add_fusion, f32[512,720]{0,1:T(8,128)S(1)} %fusion.7, bf16[512,32]{0,1:T(8,128)(2,1)S(1)} %convolution_convert_fusion.2, ...), kind=kOutput, calls=%fused_computation.23 | convolution fusion | flops 29491200 | bytes 8188928 | tf_op jit(solution)/shard_map/dot_general | solution.py:15
  82.5 0.0 copy-start.7
  82.5 0.0 copy-start.9
  82.6 0.2 fusion.25
  82.8 0.3 fusion.13
  83.0 0.7 copy-done.7
  83.7 0.1 copy-done.11
  83.8 0.3 fusion.24
  84.1 0.0 copy-done.9
  84.1 0.7 pad_maximum_fusion.1
  84.8 0.4 collective-permute-start
  85.2 0.3 fusion.45
  85.5 0.0 copy-start.8
  85.5 0.3 fusion.26
  85.8 0.3 fusion.27
  86.2 0.7 copy-done.8
  86.9 8.4 %fusion = f32[512,2880,1]{0,1,2:T(8,128)S(1)} fusion(bf16[1,2,720,2880]{3,2,1,0:T(8,128)(2,1)} %param.16, f32[512,1,720]{0,2,1:T(8,128)} %copy-done.9, f32[512,1,720]{0,2,1:T(8,128)S(1)} %copy-done.8, f32[2,720]{1,0:T(2,128)S(1)} %bitcast.113), kind=kOutput, calls=%fused_computation | convolution fusion | flops 4248944640 | bytes 17147520 | tf_op jit(solution)/shard_map/rjf,jfd->rd/dot_general | solution.py:497
  95.3 1.0 fusion.11.part_ref
  96.3 0.0 collective-permute-done
  96.3 0.9 fusion.33
  97.2 1.9 %fusion.14 = f32[32,1440]{1,0:T(8,128)S(1)} fusion(bf16[2880,512]{1,0:T(8,128)(2,1)} %copy-done.5, s32[]{:T(128)S(6)} %select_n.13, bf16[512,64]{0,1:T(8,128)(2,1)S(1)} %fusion.33), kind=kOutput, calls=%fused_computation.19 | convolution fusion | flops 47185920 | bytes 1691652 | tf_op jit(solution)/shard_map/dot_general | solution.py:15
  99.1 1.9 %fusion.16 = f32[32,1440]{1,0:T(8,128)S(1)} fusion(bf16[2880,512]{1,0:T(8,128)(2,1)} %copy-done.1, s32[]{:T(128)S(6)} %select_n.13, bf16[512,64]{0,1:T(8,128)(2,1)S(1)} %fusion.33), kind=kOutput, calls=%fused_computation.21 | convolution fusion | flops 47185920 | bytes 1691652 | tf_op jit(solution)/shard_map/dot_general | solution.py:15
  101.1 34.0 %shard_map.156 = (bf16[1440,128]{1,0:T(8,128)(2,1)S(1)}, f32[64,1440]{1,0:T(8,128)S(1)}, f32[96,720]{1,0:T(8,128)S(1)}) custom-call(bf16[2880,512]{1,0:T(8,128)(2,1)S(1)} %fusion.11.part_ref, bf16[64,1440]{1,0:T(8,128)(2,1)S(1)} %fusion.28.wide_ref, bf16[96,720]{1,0:T(8,128)(2,1)S(1)} %fusion.29.thin_ref), custom_call_target="tpu_custom_call" | custom-call | tf_op jit(solution)/shard_map/pallas_call | solution.py:323
  135.1 0.7 slice_bitcast_fusion.6
  135.8 0.8 copy.26
  136.6 0.8 slice_bitcast_fusion.4
  137.4 0.7 copy.31
  (13 shorter events, 0.2 us)
Async XLA Ops:
  0.6 62.0 %copy-start = (bf16[1,2880,32]{1,2,0:T(8,128)(2,1)S(1)}, bf16[1,2880,32]{1,2,0:T(8,128)(2,1)}, u32[]{:S(2)}) copy-start(bf16[1,2880,32]{1,2,0:T(8,128)(2,1)} %param.20) | copy-start | bytes 552964
  2.3 1.0 copy-start.3
  3.3 1.0 copy-start.4
  61.0 1.6 %copy-start.2 = (bf16[2880,512]{1,0:T(8,128)(2,1)}, bf16[2880,512]{1,0:T(8,128)(2,1)S(1)}, u32[]{:S(2)}) copy-start(bf16[2880,512]{1,0:T(8,128)(2,1)S(1)} %get-tuple-element.12) | copy-start | bytes 8847364
  62.6 16.0 %copy-start.1 = (bf16[2880,512]{1,0:T(8,128)(2,1)}, bf16[2880,512]{1,0:T(8,128)(2,1)S(1)}, u32[]{:S(2)}) copy-start(bf16[2880,512]{1,0:T(8,128)(2,1)S(1)} %get-tuple-element.13) | copy-start | bytes 8847364
  63.2 3.2 %copy-start.15 = (f32[1,2,720]{2,1,0:T(2,128)S(1)}, f32[1,2,720]{2,1,0:T(2,128)}, u32[]{:S(2)}) copy-start(f32[1,2,720]{2,1,0:T(2,128)} %param.17) | copy-start | bytes 17284
  63.2 3.2 %copy-start.14 = (f32[1,2880]{1,0:T(1,128)S(1)}, f32[1,2880]{1,0:T(1,128)}, u32[]{:S(2)}) copy-start(f32[1,2880]{1,0:T(1,128)} %param.19) | copy-start | bytes 34564
  66.5 2.5 %copy-start.12 = (bf16[1,32,2880]{2,1,0:T(8,128)(2,1)S(1)}, bf16[1,32,2880]{2,1,0:T(8,128)(2,1)}, u32[]{:S(2)}) copy-start(bf16[1,32,2880]{2,1,0:T(8,128)(2,1)} %param.23) | copy-start | bytes 552964
  66.5 9.6 %slice-start = ((s8[8478720]{0:T(1024)(128)(4,1)}), s8[90112]{0:T(1024)(128)(4,1)S(1)}, s32[]{:S(2)}) async-start(s8[8478720]{0:T(1024)(128)(4,1)} %bitcast.114), calls=%async_computation | async-start | bytes 180224
  69.0 1.6 %copy-start.5 = (bf16[2880,512]{1,0:T(8,128)(2,1)}, bf16[2880,512]{1,0:T(8,128)(2,1)S(1)}, u32[]{:S(2)}) copy-start(bf16[2880,512]{1,0:T(8,128)(2,1)S(1)} %multiply_convert_fusion.1) | copy-start | bytes 8847364
  69.0 7.1 %slice-start.1 = ((s8[8478720]{0:T(1024)(128)(4,1)}), s8[4194304]{0:T(1024)(128)(4,1)S(1)}, s32[]{:S(2)}) async-start(s8[8478720]{0:T(1024)(128)(4,1)} %bitcast.114), calls=%async_computation.1 | async-start | bytes 8388608
  70.6 5.5 %copy-start.10 = (f32[512,720]{0,1:T(8,128)S(1)}, f32[512,720]{0,1:T(8,128)}, u32[]{:S(2)}) copy-start(f32[512,720]{0,1:T(8,128)} %fusion.34) | copy-start | bytes 4423684
  70.6 5.5 %slice-start.2 = ((s8[8478720]{0:T(1024)(128)(4,1)}), s8[4194304]{0:T(1024)(128)(4,1)S(1)}, s32[]{:S(2)}) async-start(s8[8478720]{0:T(1024)(128)(4,1)} %bitcast.114), calls=%async_computation.2 | async-start | bytes 8388608
  76.2 2.5 %copy-start.6 = (f32[512,720]{0,1:T(8,128)S(1)}, f32[512,720]{0,1:T(8,128)}, u32[]{:S(2)}) copy-start(f32[512,720]{0,1:T(8,128)} %fusion.35) | copy-start | bytes 4423684
  78.6 2.5 %copy-start.13 = (bf16[1,720,32]{1,2,0:T(8,128)(2,1)S(1)}, bf16[1,720,32]{1,2,0:T(8,128)(2,1)}, u32[]{:S(2)}) copy-start(bf16[1,720,32]{1,2,0:T(8,128)(2,1)} %param.22) | copy-start | bytes 138244
  82.5 1.2 copy-start.7
  82.5 1.6 %copy-start.9 = (f32[512,1,720]{0,2,1:T(8,128)}, f32[512,1,720]{0,2,1:T(8,128)S(1)}, u32[]{:S(2)}) copy-start(f32[512,1,720]{0,2,1:T(8,128)S(1)} %get-tuple-element.36) | copy-start | bytes 4423684
  82.8 1.0 copy-start.11
  84.8 11.5 %collective-permute-start = (bf16[64,512]{1,0:T(8,128)(2,1)}, bf16[64,512]{1,0:T(8,128)(2,1)}, u32[]{:S(2)}, u32[]{:S(2)}) collective-permute-start(bf16[64,512]{1,0:T(8,128)(2,1)} %pad_maximum_fusion.1), channel_id=1, source_target_pairs={{0,1},{1,0},{2,3},{3,2},{4,5},{5,4},{6,7},{7,6},{8,9},{9,8},{10,11... | collective-permute-start | bytes 196616 | tf_op jit(solution)/shard_map/ppermute | solution.py:489
  85.5 1.4 %copy-start.8 = (f32[512,1,720]{0,2,1:T(8,128)S(1)}, f32[512,1,720]{0,2,1:T(8,128)}, u32[]{:S(2)}) copy-start(f32[512,1,720]{0,2,1:T(8,128)} %copy-done.7) | copy-start | bytes 4423684
